TPU v7x, 32 devices: a whole 2x2x4 slice. The times are simulated.
32 devices in a mesh: dp: 16 (over z, x, core), tensor: 2 (over y).
Axes of the slice: x: 2, y: 2, z: 4, core: 2. Of those that a mesh axis runs over, the one named last changes fastest.
Arguments:
- block_input: bfloat16 [16384, 1536], P('dp'), may hold values from -6 to 6
- norm_gain: float32 [1536], replicated, may hold values from 0.5 to 1.5
- z_weight: bfloat16 [1536, 3072], P(None, 'tensor'), may hold values from -0.15625 to 0.15625
- x_weight: bfloat16 [1536, 3072], P(None, 'tensor'), may hold values from -0.15625 to 0.15625
- bc_weight: bfloat16 [1536, 256], replicated, may hold values from -0.15625 to 0.15625
- dt_weight: bfloat16 [1536, 48], P(None, 'tensor'), may hold values from -0.15625 to 0.15625
- x_conv: float32 [4, 3072], P(None, 'tensor'), may hold values from -0.5 to 0.5
- x_conv_bias: float32 [3072], P('tensor'), may hold values from -0.5 to 0.5
- bc_conv: float32 [4, 256], replicated, may hold values from -0.5 to 0.5
- bc_conv_bias: float32 [256], replicated, may hold values from -0.5 to 0.5
- dt_bias: float32 [48], P('tensor'), may hold values from -7 to -2.3
- a_log: float32 [48], P('tensor'), may hold values from 0 to 2.77
- d_skip: float32 [48], P('tensor'), may hold values from 0.5 to 1.5
- gated_gain: float32 [3072], P('tensor'), may hold values from 0.5 to 1.5
- out_weight: bfloat16 [3072, 1536], P('tensor'), may hold values from -0.109375 to 0.109375
- out_cotangent: bfloat16 [16384, 1536], P('dp'), may hold values from -6 to 6
Outputs:
- block_output: bfloat16 [16384, 1536], P('dp')
- input_grad: bfloat16 [16384, 1536], P('dp')
- norm_gain_grad: float32 [1536], P(('dp', 'tensor'))
- z_weight_grad: float32 [1536, 3072], P('dp', 'tensor')
- x_weight_grad: float32 [1536, 3072], P('dp', 'tensor')
- bc_weight_grad: float32 [1536, 256], P(('dp', 'tensor'))
- dt_weight_grad: float32 [1536, 48], P('dp', 'tensor')
- x_conv_grad: float32 [4, 3072], P(None, 'tensor')
- x_conv_bias_grad: float32 [3072], P('tensor')
- bc_conv_grad: float32 [4, 256], P(None, ('dp', 'tensor'))
- bc_conv_bias_grad: float32 [256], P(('dp', 'tensor'))
- dt_bias_grad: float32 [48], P('tensor')
- a_log_grad: float32 [48], P('tensor')
- d_skip_grad: float32 [48], P('tensor')
- gated_gain_grad: float32 [3072], P('tensor')
- out_weight_grad: float32 [3072, 1536], P('tensor', 'dp')
All inputs are finite; a program needn't handle non-finite values.
Results may differ from a plain program's by a relative error of at most 0.0076.
Values sent between devices are 32-bit elements; how exact they have to be, the bound alone decides.
No kernel may reach another device: no remote copies, remote signals or barrier semaphores. Data moves between devices by JAX's collectives and lax.ppermute only.
A program may use at most 256 MiB of HBM per device.

v0:
```python
import math

import jax
import jax.numpy as jnp
from jax import lax
from jax.sharding import PartitionSpec as P

SPAN = 256
LEN = 1024


EPS = 1e-05
HIGH = lax.Precision.HIGHEST


def scan_heads(inputs_x, steps_dt, decay_a, skip_d, b_mat, c_mat):
    seq_count, length, head_count, head_dim = inputs_x.shape
    span_count = length // SPAN
    state_dim = b_mat.shape[-1]
    weighted = (inputs_x * steps_dt[..., None]).reshape(
        seq_count, span_count, SPAN, head_count, head_dim
    )
    rates = (steps_dt * decay_a).reshape(seq_count, span_count, SPAN, head_count)
    within = jnp.cumsum(rates, axis=2)
    b_blocks = b_mat.reshape(seq_count, span_count, SPAN, state_dim)
    c_blocks = c_mat.reshape(seq_count, span_count, SPAN, state_dim)
    scores = jnp.einsum("acln,acsn->acls", c_blocks, b_blocks, precision=HIGH)
    row_index = lax.broadcasted_iota(jnp.int32, (SPAN, SPAN), 0)
    col_index = lax.broadcasted_iota(jnp.int32, (SPAN, SPAN), 1)
    causal = row_index >= col_index
    within_heads = jnp.moveaxis(within, 3, 2)
    log_gaps = within_heads[..., :, None] - within_heads[..., None, :]
    decays = jnp.exp(jnp.where(causal, log_gaps, -jnp.inf))
    mixing = decays * scores[:, :, None]
    diag_out = jnp.einsum("achls,acshp->aclhp", mixing, weighted, precision=HIGH)
    to_end = jnp.exp(within[:, :, -1:, :] - within)
    scaled = weighted * to_end[..., None]
    states = jnp.einsum("acsn,acshp->achpn", b_blocks, scaled, precision=HIGH)
    span_decay = jnp.exp(within[:, :, -1, :])

    def carry_step(carried, pieces):
        decay_now, state_now = pieces
        return (decay_now[:, :, None, None] * carried + state_now, carried)

    initial = jnp.zeros((seq_count, head_count, head_dim, state_dim), jnp.float32)
    last_state, before = lax.scan(
        carry_step, initial, (jnp.moveaxis(span_decay, 1, 0), jnp.moveaxis(states, 1, 0))
    )
    before = jnp.moveaxis(before, 0, 1)
    off_out = (
        jnp.einsum("acln,achpn->aclhp", c_blocks, before, precision=HIGH)
        * jnp.exp(within)[..., None]
    )
    result = (diag_out + off_out).reshape(seq_count, length, head_count, head_dim)
    return result + skip_d[:, None] * inputs_x


def take_heads(values, group_index, head_block, along):
    return lax.dynamic_slice_in_dim(values, group_index * head_block, head_block, along)


def join_heads(stacked):
    moved = jnp.moveaxis(stacked, 0, 2)
    return moved.reshape(moved.shape[:2] + (-1,) + moved.shape[4:])


def ssd_forward(x_heads, steps_dt, decay_a, d_skip, b_mat, c_mat, head_block):
    head_count = x_heads.shape[2]

    def one_group(group_index):
        return scan_heads(
            take_heads(x_heads, group_index, head_block, 2),
            take_heads(steps_dt, group_index, head_block, 2),
            take_heads(decay_a, group_index, head_block, 0),
            take_heads(d_skip, group_index, head_block, 0),
            b_mat,
            c_mat,
        )

    stacked = lax.map(one_group, jnp.arange(head_count // head_block, dtype=jnp.int32))
    return join_heads(stacked)


def ssd_backward(x_heads, steps_dt, decay_a, d_skip, b_mat, c_mat, y_grad, head_block):
    head_count = x_heads.shape[2]

    def one_group(carried, group_index):
        inputs = (
            take_heads(x_heads, group_index, head_block, 2),
            take_heads(steps_dt, group_index, head_block, 2),
            take_heads(decay_a, group_index, head_block, 0),
            take_heads(d_skip, group_index, head_block, 0),
        )
        outputs, pull = jax.vjp(scan_heads, *inputs, b_mat, c_mat)
        grads = pull(take_heads(y_grad, group_index, head_block, 2))
        return ((carried[0] + grads[4], carried[1] + grads[5]), grads[:4])

    initial = (jnp.zeros_like(b_mat), jnp.zeros_like(c_mat))
    summed, stacked = lax.scan(
        one_group, initial, jnp.arange(head_count // head_block, dtype=jnp.int32)
    )
    return (
        join_heads(stacked[0]),
        join_heads(stacked[1]),
        stacked[2].reshape(-1),
        stacked[3].reshape(-1),
        summed[0],
        summed[1],
    )


def causal_conv(values, kernel, offsets):
    taps = kernel.shape[0]
    length = values.shape[1]
    padded = jnp.pad(values, ((0, 0), (taps - 1, 0), (0, 0)))
    summed = offsets + jnp.zeros_like(values)
    for offset in range(taps):
        summed = summed + kernel[offset] * padded[:, offset : offset + length]
    return jax.nn.silu(summed)


def conv_section(x_pre, bc_pre, x_conv, x_conv_bias, bc_conv, bc_conv_bias):
    return (causal_conv(x_pre, x_conv, x_conv_bias), causal_conv(bc_pre, bc_conv, bc_conv_bias))


def times_transposed(left, right):
    return lax.dot_general(
        left, right, (((1,), (1,)), ((), ())), preferred_element_type=jnp.float32
    )


def over_rows(left, right):
    return lax.dot_general(
        left, right, (((0,), (0,)), ((), ())), preferred_element_type=jnp.float32
    )


def body(
    block_input,
    norm_gain,
    z_weight,
    x_weight,
    bc_weight,
    dt_weight,
    x_conv,
    x_conv_bias,
    bc_conv,
    bc_conv_bias,
    dt_bias,
    a_log,
    d_skip,
    gated_gain,
    out_weight,
    out_cotangent,
):
    row_count = block_input.shape[0]
    seq_count = row_count // LEN
    head_count = dt_weight.shape[1]
    inner_dim = x_weight.shape[1]
    head_dim = inner_dim // head_count
    state_dim = bc_weight.shape[1] // 2
    head_block = math.gcd(8, head_count)
    inner_total = inner_dim * lax.axis_size("tensor")
    residual = block_input.astype(jnp.float32)
    inv_rms = lax.rsqrt(jnp.mean(residual * residual, axis=1, keepdims=True) + EPS)
    unit_in = residual * inv_rms
    normed = (unit_in * norm_gain).astype(jnp.bfloat16)
    z_pre = jnp.dot(normed, z_weight, preferred_element_type=jnp.float32)
    x_pre = jnp.dot(normed, x_weight, preferred_element_type=jnp.float32).reshape(
        seq_count, LEN, inner_dim
    )
    bc_pre = jnp.dot(normed, bc_weight, preferred_element_type=jnp.float32).reshape(
        seq_count, LEN, 2 * state_dim
    )
    dt_pre = jnp.dot(normed, dt_weight, preferred_element_type=jnp.float32).reshape(
        seq_count, LEN, head_count
    )
    (x_act, bc_act), conv_pull = jax.vjp(
        conv_section, x_pre, bc_pre, x_conv, x_conv_bias, bc_conv, bc_conv_bias
    )
    dt_sum = dt_pre + dt_bias
    steps_dt = jax.nn.softplus(dt_sum)
    decay_a = -jnp.exp(a_log)
    x_heads = x_act.reshape(seq_count, LEN, head_count, head_dim)
    b_mat = bc_act[..., :state_dim]
    c_mat = bc_act[..., state_dim:]
    mixed = ssd_forward(x_heads, steps_dt, decay_a, d_skip, b_mat, c_mat, head_block).reshape(
        row_count, inner_dim
    )
    gate_act = jax.nn.silu(z_pre)
    gated = mixed * gate_act
    square_sum = lax.psum(jnp.sum(gated * gated, axis=1, keepdims=True), "tensor")
    gate_rms = lax.rsqrt(square_sum / inner_total + EPS)
    gated_unit = gated * gate_rms
    mixer_out = (gated_unit * gated_gain).astype(jnp.bfloat16)
    partial_out = jnp.dot(mixer_out, out_weight, preferred_element_type=jnp.float32)
    block_output = (residual + lax.psum(partial_out, "tensor")).astype(jnp.bfloat16)
    mixer_grad = times_transposed(out_cotangent, out_weight)
    out_weight_part = over_rows(mixer_out, out_cotangent)
    gated_gain_part = jnp.sum(mixer_grad * gated_unit, axis=0)
    unit_grad = mixer_grad * gated_gain
    row_dot = lax.psum(jnp.sum(unit_grad * gated_unit, axis=1, keepdims=True), "tensor")
    gated_grad = gate_rms * (unit_grad - gated_unit * (row_dot / inner_total))
    mixed_grad = (gated_grad * gate_act).reshape(seq_count, LEN, head_count, head_dim)
    gate_sig = jax.nn.sigmoid(z_pre)
    z_grad = (gated_grad * mixed * (gate_sig + z_pre * gate_sig * (1.0 - gate_sig))).astype(
        jnp.bfloat16
    )
    x_heads_grad, dt_grad, a_grad, d_skip_part, b_grad, c_grad = ssd_backward(
        x_heads, steps_dt, decay_a, d_skip, b_mat, c_mat, mixed_grad, head_block
    )
    dt_pre_grad = dt_grad * jax.nn.sigmoid(dt_sum)
    dt_bias_part = jnp.sum(dt_pre_grad, axis=(0, 1))
    a_log_part = a_grad * decay_a
    conv_grads = conv_pull(
        (x_heads_grad.reshape(seq_count, LEN, inner_dim), jnp.concatenate((b_grad, c_grad), axis=2))
    )
    x_pre_low = conv_grads[0].reshape(row_count, inner_dim).astype(jnp.bfloat16)
    bc_pre_low = conv_grads[1].reshape(row_count, 2 * state_dim).astype(jnp.bfloat16)
    dt_pre_low = dt_pre_grad.reshape(row_count, head_count).astype(jnp.bfloat16)
    normed_grad = (
        times_transposed(z_grad, z_weight)
        + times_transposed(x_pre_low, x_weight)
        + times_transposed(bc_pre_low, bc_weight)
        + times_transposed(dt_pre_low, dt_weight)
    )
    z_weight_part = over_rows(normed, z_grad)
    x_weight_part = over_rows(normed, x_pre_low)
    bc_weight_part = over_rows(normed, bc_pre_low)
    dt_weight_part = over_rows(normed, dt_pre_low)
    norm_gain_part = jnp.sum(normed_grad * unit_in, axis=0)
    in_unit_grad = normed_grad * norm_gain
    input_part = inv_rms * (
        in_unit_grad - unit_in * jnp.mean(in_unit_grad * unit_in, axis=1, keepdims=True)
    )
    input_grad = (out_cotangent.astype(jnp.float32) + lax.psum(input_part, "tensor")).astype(
        jnp.bfloat16
    )
    norm_gain_grad, bc_weight_grad, bc_conv_grad, bc_conv_bias_grad = (
        lax.psum_scatter(norm_gain_part, ("dp", "tensor"), scatter_dimension=0, tiled=True),
        lax.psum_scatter(bc_weight_part, ("dp", "tensor"), scatter_dimension=0, tiled=True),
        lax.psum_scatter(conv_grads[4], ("dp", "tensor"), scatter_dimension=1, tiled=True),
        lax.psum_scatter(conv_grads[5], ("dp", "tensor"), scatter_dimension=0, tiled=True),
    )
    x_conv_grad, x_conv_bias_grad, dt_bias_grad, a_log_grad, d_skip_grad, gated_gain_grad = (
        lax.psum(
            (conv_grads[2], conv_grads[3], dt_bias_part, a_log_part, d_skip_part, gated_gain_part),
            "dp",
        )
    )
    z_weight_grad, x_weight_grad, dt_weight_grad, out_weight_grad = (
        lax.psum_scatter(z_weight_part, "dp", scatter_dimension=0, tiled=True),
        lax.psum_scatter(x_weight_part, "dp", scatter_dimension=0, tiled=True),
        lax.psum_scatter(dt_weight_part, "dp", scatter_dimension=0, tiled=True),
        lax.psum_scatter(out_weight_part, "dp", scatter_dimension=1, tiled=True),
    )
    return (
        block_output,
        input_grad,
        norm_gain_grad,
        z_weight_grad,
        x_weight_grad,
        bc_weight_grad,
        dt_weight_grad,
        x_conv_grad,
        x_conv_bias_grad,
        bc_conv_grad,
        bc_conv_bias_grad,
        dt_bias_grad,
        a_log_grad,
        d_skip_grad,
        gated_gain_grad,
        out_weight_grad,
    )


def solution(mesh):
    in_specs = (
        P("dp", None),
        P(),
        P(None, "tensor"),
        P(None, "tensor"),
        P(),
        P(None, "tensor"),
        P(None, "tensor"),
        P("tensor"),
        P(),
        P(),
        P("tensor"),
        P("tensor"),
        P("tensor"),
        P("tensor"),
        P("tensor", None),
        P("dp", None),
    )
    out_specs = (
        P("dp", None),
        P("dp", None),
        P(("dp", "tensor")),
        P("dp", "tensor"),
        P("dp", "tensor"),
        P(("dp", "tensor"), None),
        P("dp", "tensor"),
        P(None, "tensor"),
        P("tensor"),
        P(None, ("dp", "tensor")),
        P(("dp", "tensor")),
        P("tensor"),
        P("tensor"),
        P("tensor"),
        P("tensor"),
        P("tensor", "dp"),
    )
    return jax.shard_map(body, mesh=mesh, in_specs=in_specs, out_specs=out_specs, check_vma=False)
```

profile of v0, /device:TPU:14, one launch (start us, length us, event | category | flops | bytes accessed | tf_op | source)
XLA Modules:
  0.0 1214.0 jit_solution(9916861833687394812)
XLA Ops:
  23.3 6.6 fusion.97
  29.9 6.6 copy.160
  47.7 119.6 %while.121 = (s32[]{:T(128)}, f32[3,1,1024,8,64]{2,4,3,1,0:T(8,128)}, s32[3]{0:T(128)S(1)}, f32[1,1024,24,64]{1,3,2,0:T(8,128)}, f32[1,1024,24]{1,2,0:T(8,128)},...) while((s32[]{:T(128)}, ...), condition=%wide.region_6.7_spmd, body=%wide.region_1.6_spmd.sunk | while | flops 3232063488 | bytes 52303232 | solution.py:80
  62.2 7.2 while.125
  69.5 10.8 fusion.225
  102.0 7.2 while.125
  109.3 10.8 fusion.225
  141.8 7.2 while.125
  149.1 10.8 fusion.225
  167.3 6.6 copy.162
  173.9 12.8 %multiply_reduce_fusion.10 = (f32[1024]{0:T(1024)S(1)}, f32[1024,1536]{1,0:T(8,128)}, f32[1024,1536]{1,0:T(8,128)}) fusion(f32[1024,1536]{1,0:T(8,128)} %copy.162, bf16[1024,1536]{1,0:T(8,128)(2,1)} %copy-done.9, bf16[1536,1536]{1,0:T(8,128)(2,1)} %param.28), kind=kOutput, calls=%fused_computation.170 | convolution fusion | flops 4842847232 | bytes 26742784 | tf_op jit(solution)/shard_map/dot_general | solution.py:168
  191.7 11.7 multiply_reduce_fusion.4
  208.3 13.4 %multiply_convert_fusion = (bf16[1024,1536]{1,0:T(8,128)(2,1)}, f32[1024,1536]{1,0:T(8,128)}) fusion(f32[1024,1536]{1,0:T(8,128)} %copy.162, f32[1024,1536]{1,0:T(8,128)} %get-tuple-element.1053, f32[1024]{0:T(1024)S(1)} %bitcast.601, f32[1024,1536]{1,0:T(8,128)} %get-tuple-element.1022, f32[1024,1536]{1,0:T(8,128)} %get-tuple-element.1054, ...), kind=kLoop, calls=%fused_computation.166 | loop fusion | flops 25165824 | bytes 34617344 | tf_op jit(solution)/shard_map/convert_element_type | solution.py:206
  221.7 6.7 copy.164
  232.3 389.6 %while.124 = (s32[]{:T(128)}, f32[1,1024,128]{2,1,0:T(8,128)}, f32[1,1024,128]{2,1,0:T(8,128)}, f32[3,1,1024,8,64]{2,4,3,1,0:T(8,128)}, f32[3,1,1024,8]{2,3,1,0:...) while((s32[]{:T(128)}, f32[1,1024,128]{2,1,0:T(8,128)}, ...), condition=%wide.region_31.32_spmd.clone, body=%wide.region_12.31_spmd.clone.sunk | while | flops 8895913984 | bytes 121057928 | solution.py:99
  271.9 7.2 while.126
  289.7 7.8 while.127
  307.4 13.8 %fusion.245 = (f32[4,8,256]{2,1,0:T(8,128)S(1)}, f32[4,8,256]{2,1,0:T(8,128)S(1)}, f32[4,256,256]{2,1,0:T(8,128)}) fusion(f32[4,256,256]{2,1,0:T(8,128)} %get-tuple-element.1616, f32[4,8,256]{2,1,0:T(8,128)S(1)} %bitcast_add_fusion.26, pred[256,256]{1,0:T(8,128)(4,1)S(1)} %iota_compare_fusion.5, f32[4,256,8,64]{1,0,3,2:T(4,128)} %reshape.1101, ...), kind=kOutput, calls=%fused_computation.58.clone.1 | convolution fusion | flops 1629208576 | bytes 6455296 | tf_op jit(solution)/shard_map/while/body/eval_jaxpr/transpose(jvp(achls,acshp->aclhp))/dot_general | solution.py:35
  321.3 9.9 reduce-window.74
  331.5 8.5 fusion.252
  352.3 5.4 fusion.250
  391.5 7.2 while.126
  409.3 7.8 while.127
  427.0 13.8 %fusion.245 = (f32[4,8,256]{2,1,0:T(8,128)S(1)}, f32[4,8,256]{2,1,0:T(8,128)S(1)}, f32[4,256,256]{2,1,0:T(8,128)}) fusion(f32[4,256,256]{2,1,0:T(8,128)} %get-tuple-element.1616, f32[4,8,256]{2,1,0:T(8,128)S(1)} %bitcast_add_fusion.26, pred[256,256]{1,0:T(8,128)(4,1)S(1)} %iota_compare_fusion.5, f32[4,256,8,64]{1,0,3,2:T(4,128)} %reshape.1101, ...), kind=kOutput, calls=%fused_computation.58.clone.1 | convolution fusion | flops 1629208576 | bytes 6455296 | tf_op jit(solution)/shard_map/while/body/eval_jaxpr/transpose(jvp(achls,acshp->aclhp))/dot_general | solution.py:35
  440.9 9.9 reduce-window.74
  451.1 8.5 fusion.252
  512.4 7.2 while.126
  530.2 7.8 while.127
  547.9 13.8 %fusion.245 = (f32[4,8,256]{2,1,0:T(8,128)S(1)}, f32[4,8,256]{2,1,0:T(8,128)S(1)}, f32[4,256,256]{2,1,0:T(8,128)}) fusion(f32[4,256,256]{2,1,0:T(8,128)} %get-tuple-element.1616, f32[4,8,256]{2,1,0:T(8,128)S(1)} %bitcast_add_fusion.26, pred[256,256]{1,0:T(8,128)(4,1)S(1)} %iota_compare_fusion.5, f32[4,256,8,64]{1,0,3,2:T(4,128)} %reshape.1101, ...), kind=kOutput, calls=%fused_computation.58.clone.1 | convolution fusion | flops 1629208576 | bytes 6455296 | tf_op jit(solution)/shard_map/while/body/eval_jaxpr/transpose(jvp(achls,acshp->aclhp))/dot_general | solution.py:35
  561.8 9.9 reduce-window.74
  572.0 8.5 fusion.252
  592.8 5.4 fusion.250
  627.0 10.4 fusion.112
  637.4 6.7 copy.166
  644.2 14.3 %multiply_reduce_fusion.7 = (f32[1536]{0:T(1024)S(1)}, f32[1536]{0:T(1024)S(1)}, f32[1536]{0:T(1024)S(1)}, f32[1536]{0:T(1024)S(1)}, f32[1536]{0:T(1024)S(1)}, /*index=5*/f32[1,1024,1536]{2,1,0:T(8,128)S(1)}) fusion(f32[1,1024,1536]{2,1,0:T(8,128)} %bitcast.580, f32[1024,1536]{1,0:T(8,128)} %copy-done.7, f32[1,1024,1536]{2,1,0:T(8,128)} %get-tuple-element.1026, ...), kind=kLoop, calls=%fused_computation.162 | loop fusion | flops 28303872 | bytes 31488000 | tf_op jit(solution)/shard_map/transpose(jvp())/reduce_sum | solution.py:118
  658.5 6.0 broadcast_multiply_fusion.1
  664.5 6.2 fusion.99
  670.8 8.1 fusion.126
  683.6 7.0 fusion.125
  703.1 10.0 fusion.129
  713.2 11.1 fusion.111
  724.4 10.6 fusion.128
  735.9 41.3 %all-reduce.23 = (f32[1536]{0:T(1024)S(1)}, f32[4,256]{1,0:T(4,128)S(1)}, f32[256]{0:T(256)S(1)}) all-reduce(f32[1536]{0:T(1024)S(1)} %get-tuple-element.901, f32[4,256]{1,0:T(4,128)S(1)} %pad_add_fusion.7, f32[256]{0:T(256)S(1)} %get-tuple-element.908), channel_id=2, replica_groups=mesh['dp'=16,'tensor'=2] {'dp','tensor'}, use_global_device_ids=true, to_apply=%region_35.36.clone | all-reduce | flops 2816 | bytes 22528
  778.4 47.0 %all-reduce.24 = (f32[4,1536]{1,0:T(4,128)}, f32[1536]{0:T(1024)}, f32[24]{0:T(128)}, f32[24]{0:T(128)}, f32[24]{0:T(128)}, /*index=5*/f32[1536]{0:T(1024)}) all-reduce(f32[4,1536]{1,0:T(4,128)S(1)} %pad_add_fusion.6, f32[1536]{0:T(1024)S(1)} %get-tuple-element.903, ...), channel_id=1, replica_groups=mesh['dp'=16,'tensor'=2] {'dp'}, use_global_device_ids=true, to_apply=%region_44.45 | all-reduce | flops 9288 | bytes 74304 | tf_op jit(solution)/shard_map/psum | solution.py:246
  827.5 165.9 %all-reduce.28.cloned.1.call-done = (f32[1024,1536]{1,0:T(8,128)}, f32[1024,1536]{1,0:T(8,128)}) async-done(((f32[1024,1536]{1,0:T(8,128)}, f32[1024,1536]{1,0:T(8,128)}), (f32[1024,1536]{1,0:T(8,128)}, f32[1024,1536]{1,0:T(8,128)})) %all-reduce.28.cloned.1.call-update) | async-done | bytes 12582928 | tf_op jit(solution)/shard_map/psum | solution.py:197
  993.5 13.2 %fusion.93 = (bf16[1024,1536]{1,0:T(8,128)(2,1)}, bf16[1024,1536]{1,0:T(8,128)(2,1)}) fusion(f32[1024,1536]{1,0:T(8,128)} %get-tuple-element.1011, bf16[1024,1536]{1,0:T(8,128)(2,1)} %param.26, f32[1024,1536]{1,0:T(8,128)} %get-tuple-element.1012, bf16[1024,1536]{1,0:T(8,128)(2,1)} %param.41), kind=kLoop, calls=%fused_computation.151 | loop fusion | flops 9437184 | bytes 25165824 | tf_op jit(solution)/shard_map/convert_element_type | solution.py:197
  1006.7 83.5 %reduce-scatter.15.cloned.1.call-done = f32[1536,96]{0,1:T(8,128)} async-done(((f32[1536,1536]{0,1:T(8,128)}), f32[1536,96]{0,1:T(8,128)}) %reduce-scatter.15.cloned.1.call-update) | async-done | bytes 589840 | tf_op jit(solution)/shard_map/reduce_scatter | solution.py:255
  1090.2 116.2 %reduce-scatter.9.cloned.1.call-done = f32[96,1536]{1,0:T(8,128)} async-done(((f32[1536,1536]{1,0:T(8,128)}), f32[96,1536]{1,0:T(8,128)}) %reduce-scatter.9.cloned.1.call-update) | async-done | bytes 589840 | tf_op jit(solution)/shard_map/reduce_scatter | solution.py:252
  (583 shorter events, 401.7 us)
Async XLA Ops:
  8.0 818.0 %reduce-scatter.17.cloned.1.call-start = ((), (), s32[]{:S(2)}) async-start(), calls=%async_computation.9 | async-start | bytes 835584
  23.1 6.7 copy-start.7
  23.2 6.7 copy-start.24
  23.2 6.6 copy-start.26
  23.2 6.6 copy-start.28
  29.9 6.7 copy-start.21
  29.9 6.6 copy-start.51
  29.9 10.8 copy-start.53
  62.2 7.3 copy-start.20
  69.4 10.9 copy-start.10
  102.0 7.3 copy-start.20
  109.1 10.9 copy-start.10
  141.8 7.3 copy-start.20
  148.9 10.9 copy-start.10
  173.9 17.8 %copy-start.47 = (f32[1536]{0:T(1024)S(1)}, f32[1536]{0:T(1024)}, u32[]{:S(2)}) copy-start(f32[1536]{0:T(1024)} %param.39) | copy-start | bytes 18436
  191.7 16.6 %copy-start.35 = (f32[1024,1]{0,1:T(1,128)}, f32[1024,1]{0,1:T(1,128)S(1)}, u32[]{:S(2)}) copy-start(f32[1024,1]{0,1:T(1,128)S(1)} %add_rsqrt_fusion) | copy-start | bytes 12292
  251.7 14.3 %copy-start.4 = (f32[1,1024,128]{2,1,0:T(8,128)}, f32[1,1024,128]{2,1,0:T(8,128)S(1)}, u32[]{:S(2)}) copy-start(f32[1,1024,128]{2,1,0:T(8,128)S(1)} %get-tuple-element.1614) | copy-start | bytes 1572868 | tf_op jit(solution)/shard_map/while
  270.7 8.4 copy-start.16
  344.1 13.7 %copy-start.5 = (f32[1,1024,128]{2,1,0:T(8,128)S(1)}, f32[1,1024,128]{2,1,0:T(8,128)}, u32[]{:S(2)}) copy-start(f32[1,1024,128]{2,1,0:T(8,128)} %copy-done.4) | copy-start | bytes 1572868 | tf_op jit(solution)/shard_map/while
  351.0 14.1 %copy-start.2 = (f32[4,256,8,64]{1,0,3,2:T(4,128)S(1)}, f32[4,256,8,64]{1,0,3,2:T(4,128)}, u32[]{:S(2)}) copy-start(f32[4,256,8,64]{1,0,3,2:T(4,128)} %reshape.1101) | copy-start | bytes 6291460 | tf_op jit(solution)/shard_map/while
  371.4 14.3 %copy-start.4 = (f32[1,1024,128]{2,1,0:T(8,128)}, f32[1,1024,128]{2,1,0:T(8,128)S(1)}, u32[]{:S(2)}) copy-start(f32[1,1024,128]{2,1,0:T(8,128)S(1)} %get-tuple-element.1614) | copy-start | bytes 1572868 | tf_op jit(solution)/shard_map/while
  390.4 8.4 copy-start.16
  463.7 13.7 %copy-start.5 = (f32[1,1024,128]{2,1,0:T(8,128)S(1)}, f32[1,1024,128]{2,1,0:T(8,128)}, u32[]{:S(2)}) copy-start(f32[1,1024,128]{2,1,0:T(8,128)} %copy-done.4) | copy-start | bytes 1572868 | tf_op jit(solution)/shard_map/while
  470.7 14.3 %copy-start.2 = (f32[4,256,8,64]{1,0,3,2:T(4,128)S(1)}, f32[4,256,8,64]{1,0,3,2:T(4,128)}, u32[]{:S(2)}) copy-start(f32[4,256,8,64]{1,0,3,2:T(4,128)} %reshape.1101) | copy-start | bytes 6291460 | tf_op jit(solution)/shard_map/while
  492.3 14.3 %copy-start.4 = (f32[1,1024,128]{2,1,0:T(8,128)}, f32[1,1024,128]{2,1,0:T(8,128)S(1)}, u32[]{:S(2)}) copy-start(f32[1,1024,128]{2,1,0:T(8,128)S(1)} %get-tuple-element.1614) | copy-start | bytes 1572868 | tf_op jit(solution)/shard_map/while
  511.2 8.4 copy-start.16
  584.6 13.7 %copy-start.5 = (f32[1,1024,128]{2,1,0:T(8,128)S(1)}, f32[1,1024,128]{2,1,0:T(8,128)}, u32[]{:S(2)}) copy-start(f32[1,1024,128]{2,1,0:T(8,128)} %copy-done.4) | copy-start | bytes 1572868 | tf_op jit(solution)/shard_map/while
  591.5 14.3 %copy-start.2 = (f32[4,256,8,64]{1,0,3,2:T(4,128)S(1)}, f32[4,256,8,64]{1,0,3,2:T(4,128)}, u32[]{:S(2)}) copy-start(f32[4,256,8,64]{1,0,3,2:T(4,128)} %reshape.1101) | copy-start | bytes 6291460 | tf_op jit(solution)/shard_map/while
  626.9 366.6 %all-reduce.28.cloned.1.call-start = ((), (), s32[]{:S(2)}) async-start(), calls=%async_computation.10 | async-start | bytes 25165824 | tf_op jit(solution)/shard_map/psum | solution.py:197
  637.4 6.7 copy-start.11
  644.1 14.3 %copy-start.25 = (f32[1536]{0:T(1024)S(1)}, f32[1536]{0:T(1024)}, u32[]{:S(2)}) copy-start(f32[1536]{0:T(1024)} %copy-done.24) | copy-start | bytes 18436
  644.2 14.3 %copy-start.27 = (f32[1536]{0:T(1024)S(1)}, f32[1536]{0:T(1024)}, u32[]{:S(2)}) copy-start(f32[1536]{0:T(1024)} %copy-done.26) | copy-start | bytes 18436
  644.2 14.3 %copy-start.29 = (f32[1536]{0:T(1024)S(1)}, f32[1536]{0:T(1024)}, u32[]{:S(2)}) copy-start(f32[1536]{0:T(1024)} %copy-done.28) | copy-start | bytes 18436
  644.2 14.3 %copy-start.31 = (f32[1536]{0:T(1024)S(1)}, f32[1536]{0:T(1024)}, u32[]{:S(2)}) copy-start(f32[1536]{0:T(1024)} %copy-done.30) | copy-start | bytes 18436
  670.7 8.2 copy-start.17
  670.7 8.2 copy-start.12
  670.7 8.3 copy-start.14
  670.8 8.3 copy-start.15
  683.6 7.0 copy-start.8
  683.6 7.0 copy-start.22
  683.6 7.0 copy-start.23
  683.6 7.0 copy-start.33
  698.9 307.9 %reduce-scatter.13.cloned.1.call-start = ((), (), s32[]{:S(2)}) async-start(), calls=%async_computation.7 | async-start | bytes 1622016 | tf_op jit(solution)/shard_map/reduce_scatter | solution.py:241
  703.1 303.7 %reduce-scatter.11.cloned.1.call-start = ((), (), s32[]{:S(2)}) async-start(), calls=%async_computation.6 | async-start | bytes 10027008 | tf_op jit(solution)/shard_map/reduce_scatter | solution.py:253
  713.2 377.1 %reduce-scatter.15.cloned.1.call-start = ((), (), s32[]{:S(2)}) async-start(), calls=%async_computation.8 | async-start | bytes 10027008 | tf_op jit(solution)/shard_map/reduce_scatter | solution.py:255
  724.4 482.0 %reduce-scatter.9.cloned.1.call-start = ((), (), s32[]{:S(2)}) async-start(), calls=%async_computation.5 | async-start | bytes 10027008 | tf_op jit(solution)/shard_map/reduce_scatter | solution.py:252
  735.0 43.3 %copy-start.54 = (f32[24]{0:T(128)S(1)}, f32[24]{0:T(128)}, u32[]{:S(2)}) copy-start(f32[24]{0:T(128)} %param.37) | copy-start | bytes 292
  735.0 43.3 %copy-start.46 = (f32[1536]{0:T(1024)S(1)}, f32[1536]{0:T(1024)}, u32[]{:S(2)}) copy-start(f32[1536]{0:T(1024)} %get-tuple-element.896) | copy-start | bytes 18436
  (35 other events, 113.5 us)
Sparse Core Ops, SparseCore 0:
  627.0 57.5 reduce-scatter.16
  706.4 151.9 reduce-scatter.12
  863.6 110.8 reduce-scatter.10
  979.1 111.0 reduce-scatter.14
  1095.3 111.0 reduce-scatter.8
Sparse Core Ops, SparseCore 1:
  699.0 294.5 all-reduce.27
where the time goes:
time: 1230 us; the launch traced here: 1210 us
  waiting for transfers between devices  366 us (30%)
  matrix products  325 us (26%)
  other arithmetic  264 us (21%)
  local copies, waits for them, and re-layouts  111 us (9%)
  blocking collectives  98.2 us (8%)
  loops' own time  33.9 us (3%)
  between operations  16.5 us (1%)
    psum x1, waiting for transfers between devices, body(): lax.psum(partial_out, 'tensor')  166 us
    reduce_scatter x1, waiting for transfers between devices, body(): lax.psum_scatter(z_weight_part, 'dp', scatter_dimension=0, tiled=True)  116 us
    dot_general x9, matrix products, scan_heads(): jnp.einsum('achls,acshp->aclhp', mixing, weighted, precision=HIGH)  99.3 us
    reduce_scatter x1, waiting for transfers between devices, body(): lax.psum_scatter(out_weight_part, 'dp', scatter_dimension=1, tiled=True)  83.5 us
    dot_general x12, matrix products, scan_heads(): states = jnp.einsum('acsn,acshp->achpn', b_blocks, scaled, precision=HIGH)  51.9 us
    dot_general x12, matrix products, scan_heads(): jnp.einsum('acln,achpn->aclhp', c_blocks, before, precision=HIGH)  49.9 us
    psum x1, blocking collectives, body(): lax.psum((conv_grads[2], conv_grads[3], dt_bias_part, a_log_part, d_skip_...  47 us
    another operation x38, other arithmetic  44.4 us
  transfers between devices with their start and end apart: 6, of which 3 were waited for; matrix products, arithmetic and copies ran while one was open for 10% of the time, Pallas kernels for 0%

commit v1 on v0

v1 whole, which is shorter than its diff:
```python
import functools
import math

import jax
import jax.numpy as jnp
from jax import lax
from jax.experimental import pallas as pl
from jax.experimental.pallas import tpu as pltpu
from jax.sharding import PartitionSpec as P

SPAN = 256
LEN = 1024
EPS = 1e-05
HIGH = lax.Precision.HIGHEST
LOG2E = math.log2(math.e)
F32 = jnp.float32
BF16 = jnp.bfloat16
HALO = 8
GROUP = 32
VMEM = 56 * 1024 * 1024


class Named(dict):
    __getattr__ = dict.get
    __setattr__ = dict.__setitem__


def mm(a, b):
    return lax.dot_general(a, b, (((1,), (0,)), ((), ())), preferred_element_type=F32)


def mm_nt(a, b):
    return lax.dot_general(a, b, (((1,), (1,)), ((), ())), preferred_element_type=F32)


def mm_tn(a, b):
    return lax.dot_general(a, b, (((0,), (0,)), ((), ())), preferred_element_type=F32)


def split3(x):
    hi = x.astype(BF16)
    rest = x - hi.astype(F32)
    mid = rest.astype(BF16)
    low = (rest - mid.astype(F32)).astype(BF16)
    return hi, mid, low


def split2(x):
    hi = x.astype(BF16)
    return hi, (x - hi.astype(F32)).astype(BF16)


def side(a, b):
    return jnp.concatenate((a, b), axis=1)


def folded(x):
    half = x.shape[1] // 2
    return x[:, :half] + x[:, half:]


def fine_nn(left_pair, b):
    bh, bl = split2(b)
    depth = b.shape[0]
    return mm(left_pair, jnp.concatenate((bh, bh), axis=0)) + mm(left_pair[:, :depth], bl)


def fine_rows(left_stack, b):
    bh, bl = split2(b)
    rows = left_stack.shape[0] // 2
    both = mm(left_stack, bh)
    return both[:rows] + both[rows:] + mm(left_stack[:rows], bl)


def fine_nt(a, b):
    ah, al = split2(a)
    bh, bl = split2(b)
    return folded(mm_nt(ah, jnp.concatenate((bh, bl), axis=0))) + mm_nt(al, bh)


def iota(shape, axis):
    return lax.broadcasted_iota(jnp.int32, shape, axis)


def softplus(v):
    return jnp.maximum(v, 0.0) + jnp.log1p(jnp.exp(-jnp.abs(v)))


def three_parts(x):
    hi, mid, low = split3(x)
    lane = iota(x.shape, 1)
    parts = jnp.where(
        lane < GROUP, hi.astype(F32), jnp.where(lane < 2 * GROUP, mid.astype(F32), low.astype(F32))
    )
    return parts.astype(BF16)


def spread_matrix(block, heads, head_dim, lanes):
    shape = (lanes, heads * head_dim)
    row, col = iota(shape, 0), iota(shape, 1)
    head = block * heads + col // head_dim
    hit = (row == head) | (row == head + GROUP) | (row == head + 2 * GROUP)
    return jnp.where(hit, 1.0, 0.0).astype(BF16)


def gather_matrix(block, heads, head_dim, lanes):
    shape = (heads * head_dim, lanes)
    row, col = iota(shape, 0), iota(shape, 1)
    return jnp.where(col == block * heads + row // head_dim, 1.0, 0.0).astype(BF16)


def triangle(n, lower):
    row, col = iota((n, n), 0), iota((n, n), 1)
    return jnp.where(row >= col if lower else row <= col, 1.0, 0.0)


def pair_masks(head_dim):
    lane = iota((1, 4 * head_dim), 1) // head_dim % 2
    return [jnp.where(lane == k, 1.0, 0.0).astype(BF16) for k in range(2)]


def pair_parts(parts, head_dim, pair):
    at = slice(2 * pair * head_dim, 2 * (pair + 1) * head_dim)
    return side(parts[0][:, at], parts[1][:, at])


def conv_of(buf, taps_ref, bias_ref, rows):
    taps = taps_ref.shape[0]
    total = bias_ref[...] + taps_ref[0:1, :] * buf[HALO - taps + 1 : HALO - taps + 1 + rows, :]
    for k in range(1, taps):
        start = HALO - taps + 1 + k
        total = total + taps_ref[k : k + 1, :] * buf[start : start + rows, :]
    return total


def silu_slope(v, s):
    return s + v * s * (1.0 - s)


def steps_of(dt_pre, dt_bias_ref, a_log_ref):
    dt = softplus(dt_pre + dt_bias_ref[...])
    decay = -jnp.exp(a_log_ref[...])
    rates = dt * (decay * LOG2E)
    cum = jnp.dot(triangle(dt.shape[0], True), rates, precision=HIGH, preferred_element_type=F32)
    return dt, decay, cum


def fwd_kernel(first, heads, head_dim, refs):
    j = pl.program_id(0)
    r = refs
    rows = r.xin.shape[0]
    half = rows // 2
    states = r.bc_w.shape[1] // 2
    lanes = r.dt_w.shape[1]

    @pl.when(j == 0)
    def _():
        res = r.xin[...].astype(F32)
        inv = lax.rsqrt(jnp.mean(res * res, axis=1, keepdims=True) + EPS)
        normed = (res * inv * r.norm_gain[...]).astype(BF16)
        r.normed[...] = normed
        bc_pre = mm(normed, r.bc_w[...])
        r.bc_pre[...] = bc_pre
        buf = r.bc_buf
        buf[0:HALO, :] = jnp.zeros((HALO, 2 * states), F32) if first else r.bc_halo[...]
        buf[HALO : HALO + rows, :] = bc_pre
        r.bc_halo_out[...] = bc_pre[rows - HALO :, :]
        u = conv_of(buf, r.bc_conv, r.bc_conv_bias, rows)
        act = u * jax.nn.sigmoid(u)
        b, c = act[:, :states], act[:, states:]
        r.cb[...] = side(*split2(c))
        r.bt[...] = jnp.concatenate(split2(b.T), axis=0)
        r.scores[...] = fine_nt(c, b) * triangle(rows, True)
        dt_pre = mm(normed, r.dt_w[...])
        r.dt_pre[...] = dt_pre
        dt, decay, cum = steps_of(dt_pre, r.dt_bias, r.a_log)
        r.cum_t[...] = cum.T
        r.parts[0:rows, :] = three_parts(cum)
        r.parts[rows : 2 * rows, :] = three_parts(dt)
        r.u_out[...] = jnp.zeros_like(r.u_out)
        r.acc[...] = jnp.zeros_like(r.acc)

    width = heads * head_dim
    normed = r.normed[...]
    xp = mm(normed, r.x_w[...])
    zp = mm(normed, r.z_w[...])
    mg = mm_nt(r.cot[...], r.out_w[...])
    r.x_pre[...] = xp
    r.z_pre[...] = zp
    r.mg[...] = mg
    buf = r.x_buf
    buf[0:HALO, :] = jnp.zeros((HALO, width), F32) if first else r.x_halo[...]
    buf[HALO : HALO + rows, :] = xp
    r.x_halo_out[...] = xp[rows - HALO :, :]
    u = conv_of(buf, r.x_conv, r.x_conv_bias, rows)
    xa = u * jax.nn.sigmoid(u)
    spread = mm(r.parts[...], spread_matrix(j, heads, head_dim, lanes))
    cum_e, dt_e = spread[:rows], spread[rows:]
    w = xa * dt_e
    last = cum_e[rows - 1 : rows, :]
    scaled = w * jnp.exp2(last - cum_e)
    masks = pair_masks(head_dim)
    parts = split2(w)
    cols = []
    for pair in range(heads // 2):
        both = pair_parts(parts, head_dim, pair)
        top = bot = 0.0
        for k in range(2):
            head = 2 * pair + k
            row = r.cum_t[pl.ds(j * heads + head, 1), :]
            col = cum_e[:, head * head_dim : head * head_dim + 1]
            wk = both * masks[k]
            m = jnp.exp2(jnp.minimum(col[:half] - row[:, :half], 0.0)) * r.scores[:half, :half]
            hi, low = split2(m)
            top = top + mm(hi, wk[:half]) + mm(low, wk[:half])
            m = jnp.exp2(jnp.minimum(col[half:] - row, 0.0)) * r.scores[half:, :]
            hi, low = split2(m)
            bot = bot + mm(hi, wk) + mm(low, wk)
        cols.append(folded(jnp.concatenate((top, bot), axis=0)))
    y = side(*cols)
    if first:
        r.state_out[...] = fine_rows(r.bt[...], scaled)
    else:
        state = r.state[...]
        y = y + jnp.exp2(cum_e) * fine_nn(r.cb[...], state)
        r.state_out[...] = jnp.exp2(last) * state + fine_rows(r.bt[...], scaled)
    r.y[...] = y
    mixed = y + r.d_skip[...] * xa
    gated = mixed * (zp * jax.nn.sigmoid(zp))
    gain = gated * r.gated_gain[...]
    gb = gain.astype(BF16)
    r.gb[...] = gb
    r.u_out[...] += mm(gb, r.out_w[...])
    r.acc[0:rows, :] += gated * gated
    r.acc[rows : 2 * rows, :] += mg * gain

    @pl.when(j == pl.num_programs(0) - 1)
    def _():
        ones = jnp.ones((HALO, width), F32)
        sums = lax.dot_general(
            ones, r.acc[...], (((1,), (1,)), ((), ())), precision=HIGH, preferred_element_type=F32
        )
        r.sums[0:1, :] = sums[0:1, :rows]
        r.sums[1:2, :] = sums[0:1, rows:]
        r.sums[2:HALO, :] = jnp.zeros((HALO - 2, rows), F32)


def bwd_kernel(first, last_chunk, heads, head_dim, inner_total, refs):
    j = pl.program_id(0)
    r = refs
    rows = r.xin.shape[0]
    half = rows // 2
    states = r.bc_w.shape[1] // 2
    lanes = r.dt_w.shape[1]
    width = heads * head_dim
    taps = r.x_conv.shape[0]

    def fill(buf, halo, values, columns):
        buf[0:HALO, :] = jnp.zeros((HALO, columns), F32) if first else halo[...]
        buf[HALO : HALO + rows, :] = values

    def conv_back(buf, halo, grad, taps_ref, columns):
        buf[0:rows, :] = grad
        buf[rows : rows + HALO, :] = jnp.zeros((HALO, columns), F32) if last_chunk else halo[...]
        total = taps_ref[taps - 1 : taps, :] * grad
        for k in range(taps - 1):
            total = total + taps_ref[k : k + 1, :] * buf[taps - 1 - k : taps - 1 - k + rows, :]
        return total

    def column_sum(v):
        return jnp.sum(v, axis=0, keepdims=True)

    @pl.when(j == 0)
    def _():
        bc_pre = r.bc_pre[...]
        fill(r.bc_buf, r.bc_halo, bc_pre, 2 * states)
        u = conv_of(r.bc_buf, r.bc_conv, r.bc_conv_bias, rows)
        s = jax.nn.sigmoid(u)
        act = u * s
        r.bc_slope[...] = silu_slope(u, s)
        b, c = act[:, :states], act[:, states:]
        r.bb[...] = side(*split2(b))
        r.cb[...] = side(*split2(c))
        r.ct[...] = jnp.concatenate(split2(c.T), axis=0)
        r.scores[...] = fine_nt(b, c) * triangle(rows, False)
        dt, decay, cum = steps_of(r.dt_pre[...], r.dt_bias, r.a_log)
        r.dt[...] = dt
        r.cum_t[...] = cum.T
        r.parts[0:rows, :] = three_parts(cum)
        r.parts[rows : 2 * rows, :] = three_parts(dt)
        for ref in (r.d_scores, r.db, r.dc, r.d_cum, r.d_dt, r.ng):
            ref[...] = jnp.zeros_like(ref)
        sums = (r.sums[...] + r.sums_other[...]).T
        rms = lax.rsqrt(sums[:, 0:1] / inner_total + EPS)
        r.rows[:, 0:1] = rms
        r.rows[:, 1:2] = sums[:, 1:2] * rms / inner_total

    xp = r.x_pre[...]
    fill(r.x_buf, r.x_halo, xp, width)
    u = conv_of(r.x_buf, r.x_conv, r.x_conv_bias, rows)
    su = jax.nn.sigmoid(u)
    xa = u * su
    spread = mm(r.parts[...], spread_matrix(j, heads, head_dim, lanes))
    cum_e, dt_e = spread[:rows], spread[rows:]
    w = xa * dt_e
    last = cum_e[rows - 1 : rows, :]
    rms, row_dot = r.rows[:, 0:1], r.rows[:, 1:2]
    zp, mg, y = r.z_pre[...], r.mg[...], r.y[...]
    sz = jax.nn.sigmoid(zp)
    gate = zp * sz
    d_skip = r.d_skip[...]
    mixed = y + d_skip * xa
    gated_unit = mixed * gate * rms
    gg = rms * (mg * r.gated_gain[...] - gated_unit * row_dot)
    dy = gg * gate
    zl = (gg * mixed * silu_slope(zp, sz)).astype(BF16)
    r.z_low[...] = zl
    sums = [column_sum(mg * gated_unit), column_sum(dy * xa)]
    masks = pair_masks(head_dim)
    w_parts = split2(w)
    dy_parts = split2(dy)
    cols = []
    for pair in range(heads // 2):
        at = slice(2 * pair * head_dim, 2 * (pair + 1) * head_dim)
        w_both = pair_parts(w_parts, head_dim, pair)
        w_high = w_parts[0][:, at]
        dy_both = pair_parts(dy_parts, head_dim, pair)
        dy_high = side(dy_parts[0][:, at], dy_parts[0][:, at])
        dy_low = dy_parts[1][:, at]
        top = bot = 0.0
        for k in range(2):
            head = 2 * pair + k
            row = r.cum_t[pl.ds(j * heads + head, 1), :]
            col = cum_e[:, head * head_dim : head * head_dim + 1]
            dk, dk_high = dy_both * masks[k], dy_high * masks[k]
            dk_low = dy_low * masks[k][:, : 2 * head_dim]
            decay = jnp.exp2(jnp.minimum(row - col[:half], 0.0))
            grad = mm_nt(w_both[:half], dk_high) + mm_nt(w_high[:half], dk_low)
            r.d_scores[:half, :] += grad * decay
            hi, low = split2(decay * r.scores[:half, :])
            top = top + mm(hi, dk) + mm(low, dk)
            decay = jnp.exp2(jnp.minimum(row[:, half:] - col[half:], 0.0))
            grad = mm_nt(w_both[half:], dk_high[half:]) + mm_nt(w_high[half:], dk_low[half:])
            r.d_scores[half:, half:] += grad * decay
            hi, low = split2(decay * r.scores[half:, half:])
            bot = bot + mm(hi, dk[half:]) + mm(low, dk[half:])
        cols.append(folded(jnp.concatenate((top, bot), axis=0)))
    dw = side(*cols)
    extra = None
    if not last_chunk:
        to_end = jnp.exp2(last - cum_e)
        d_state = r.d_state[...]
        ds = fine_nn(r.bb[...], d_state) * to_end
        r.db[...] += fine_nt(w * to_end, d_state)
        dw = dw + ds
        extra = column_sum(w * ds)
    if not first:
        state = r.state[...]
        g = jnp.exp2(cum_e) * dy
        r.dc[...] += fine_nt(g, state)
        d_state_out = fine_rows(r.ct[...], g)
        if not last_chunk:
            kept = jnp.exp2(last) * d_state
            extra = extra + column_sum(kept * state)
            d_state_out = d_state_out + kept
        r.d_state_out[...] = d_state_out
    q = dy * y - w * dw
    if extra is not None:
        q = q + jnp.where(iota((rows, 1), 0) == rows - 1, 1.0, 0.0) * extra
    gather = gather_matrix(j, heads, head_dim, lanes)
    hi, mid, low = split3(q)
    r.d_cum[...] += mm(hi, gather) + mm(mid, gather) + mm(low, gather)
    hi, mid, low = split3(dw * xa)
    r.d_dt[...] += mm(hi, gather) + mm(mid, gather)
    du = (d_skip * dy + dw * dt_e) * silu_slope(u, su)
    xg = conv_back(r.x_grad_buf, r.du_halo, du, r.x_conv, width)
    r.du_halo_out[...] = du[:HALO, :]
    for k in range(taps):
        start = HALO - taps + 1 + k
        sums.append(column_sum(du * r.x_buf[start : start + rows, :]))
    sums.append(column_sum(du))
    for at, value in enumerate(sums):
        before = 0.0 if last_chunk else r.x_sums_in[at : at + 1, :]
        r.x_sums[at : at + 1, :] = value + before
    r.x_sums[len(sums) : HALO, :] = jnp.zeros((HALO - len(sums), width), F32)
    xl = xg.astype(BF16)
    r.x_low[...] = xl
    r.ng[...] += mm_nt(zl, r.z_w[...]) + mm_nt(xl, r.x_w[...])

    @pl.when(j == pl.num_programs(0) - 1)
    def _():
        hi, low = split2(r.d_scores[...] * triangle(rows, False))
        cb, bb = r.cb[...], r.bb[...]
        db = r.db[...] + folded(mm(hi, cb)) + mm(low, cb[:, :states])
        dc = r.dc[...] + folded(mm_tn(hi, bb)) + mm_tn(low, bb[:, :states])
        d_rates = jnp.dot(
            triangle(rows, False), r.d_cum[...], precision=HIGH, preferred_element_type=F32
        )
        dt = r.dt[...]
        decay = -jnp.exp(r.a_log[...])
        d_dt = d_rates * decay + r.d_dt[...]
        dtg = d_dt * jax.nn.sigmoid(r.dt_pre[...] + r.dt_bias[...])
        dtl = jnp.where(iota(dtg.shape, 1) < GROUP, dtg, 0.0).astype(BF16)
        r.dt_low[...] = dtl
        head_sums = [column_sum(dtg), column_sum(d_rates * dt) * decay]
        for at, value in enumerate(head_sums):
            before = 0.0 if last_chunk else r.head_sums_in[at : at + 1, :]
            r.head_sums[at : at + 1, :] = value + before
        r.head_sums[2:HALO, :] = jnp.zeros((HALO - 2, lanes), F32)
        du_bc = jnp.concatenate((db, dc), axis=1) * r.bc_slope[...]
        bg = conv_back(r.bc_grad_buf, r.du_bc_halo, du_bc, r.bc_conv, 2 * states)
        r.du_bc_halo_out[...] = du_bc[:HALO, :]
        bc_sums = []
        for k in range(taps):
            start = HALO - taps + 1 + k
            bc_sums.append(column_sum(du_bc * r.bc_buf[start : start + rows, :]))
        bc_sums.append(column_sum(du_bc))
        for at, value in enumerate(bc_sums):
            before = 0.0 if last_chunk else r.bc_sums_in[at : at + 1, :]
            r.bc_sums[at : at + 1, :] = value + before
        r.bc_sums[len(bc_sums) : HALO, :] = jnp.zeros((HALO - len(bc_sums), 2 * states), F32)
        bl = bg.astype(BF16)
        r.bc_low[...] = bl
        ng = r.ng[...] + mm_nt(bl, r.bc_w[...]) + mm_nt(dtl, r.dt_w[...])
        res = r.xin[...].astype(F32)
        inv = lax.rsqrt(jnp.mean(res * res, axis=1, keepdims=True) + EPS)
        unit = res * inv
        gain_sum = column_sum(ng * unit)
        r.gain_sums[0:1, :] = gain_sum if last_chunk else gain_sum + r.gain_sums_in[0:1, :]
        r.gain_sums[1:HALO, :] = jnp.zeros((HALO - 1, gain_sum.shape[1]), F32)
        iu = ng * r.norm_gain[...]
        r.in_part[...] = inv * (iu - unit * jnp.mean(iu * unit, axis=1, keepdims=True))


def run_kernel(body, grid, operands, outs, scratch, carried, flops, moved):
    names, arrays, specs = [], [], []
    for name, (array, block, index) in operands.items():
        names.append(name)
        arrays.append(array)
        specs.append(pl.BlockSpec(block, index))
    aliases = {}
    out_names = list(outs)
    for at, name in enumerate(out_names):
        if name in carried:
            aliases[len(arrays)] = at
            names.append(name + "_old")
            arrays.append(carried[name])
            specs.append(pl.BlockSpec(memory_space=pl.ANY))
    scratch_names = list(scratch)

    def kernel(*refs):
        body(Named(zip(names + out_names + scratch_names, refs)))

    given = pl.pallas_call(
        kernel,
        grid=(grid,),
        in_specs=specs,
        out_specs=[pl.BlockSpec(block, index) for _, block, index in outs.values()],
        out_shape=[shape for shape, _, _ in outs.values()],
        scratch_shapes=[pltpu.VMEM(shape, kind) for shape, kind in scratch.values()],
        input_output_aliases=aliases,
        compiler_params=pltpu.CompilerParams(
            dimension_semantics=("arbitrary",), vmem_limit_bytes=VMEM
        ),
        cost_estimate=pl.CostEstimate(flops=flops, bytes_accessed=moved, transcendentals=0),
    )(*arrays)
    return Named(zip(out_names, given))


def shape(*dims, kind=F32):
    return jax.ShapeDtypeStruct(dims, kind)


def stage_sizes(n):
    sizes = []
    while n > 1 and len(sizes) < 2 and n % 2 == 0:
        sizes.append(2)
        n //= 2
    while n > 1:
        part = 4 if n % 4 == 0 else (2 if n % 2 == 0 else n)
        sizes.append(part)
        n //= part
    return sizes


def hops(n, stride, size, step, keep):
    pairs = []
    for d in range(n):
        place = d // stride % size
        if keep(place) and 0 <= place + step < size:
            pairs.append((d, d + step * stride))
    return pairs


def line_sum(values, n, stride, size):
    place = lax.axis_index("dp") // stride % size

    def block(at):
        return lax.dynamic_index_in_dim(values, jnp.clip(at, 0, size - 1), 0, keepdims=False)

    if size == 2:
        other = lax.ppermute(
            block(1 - place), "dp", hops(n, stride, size, 1, lambda p: True)
            + hops(n, stride, size, -1, lambda p: True)
        )
        return block(place) + other
    right = left = None
    for step in range(1, size):
        send = block(size - step + place)
        send = send if right is None else send + right
        right = lax.ppermute(send, "dp", hops(n, stride, size, 1, lambda p: p <= step - 1))
        send = block(step + place - size)
        send = send if left is None else send + left
        left = lax.ppermute(send, "dp", hops(n, stride, size, -1, lambda p: p >= size - step))
    return block(place) + right + left


def doubling_sum(values, n):
    step = 1
    while step < n:
        if n % (2 * step):
            return lax.psum(values, "dp")
        values = values + lax.ppermute(values, "dp", [(d, d ^ step) for d in range(n)])
        step *= 2
    return values


def by_stage(left, n):
    sizes = stage_sizes(n)
    rows, depth = left.shape
    cut = left.reshape(tuple(reversed(sizes)) + (rows // n, depth))
    k = len(sizes)
    return jnp.transpose(cut, tuple(range(k - 1, -1, -1)) + (k, k + 1))


def scattered_product(left, right, n):
    sizes = stage_sizes(n)
    rest, depth = left.shape[-2:]
    if not sizes:
        return jnp.dot(left.reshape(-1, depth), right, preferred_element_type=F32)
    if sizes[0] != 2:
        total = jnp.dot(left.reshape(-1, depth), right, preferred_element_type=F32)
        total = total.reshape(left.shape[:-1] + (right.shape[1],))
        stride = 1
        for size in sizes:
            total = line_sum(total, n, stride, size)
            stride *= size
        return total
    place = lax.axis_index("dp") % 2

    def share(at):
        mine = lax.dynamic_index_in_dim(left, at, 0, keepdims=False).reshape(-1, depth)
        return jnp.dot(mine, right, preferred_element_type=F32)

    other = lax.ppermute(share(1 - place), "dp", [(d, d ^ 1) for d in range(n)])
    total = share(place) + other
    total = total.reshape(left.shape[1:-1] + (right.shape[1],))
    stride = 2
    for size in sizes[1:]:
        total = line_sum(total, n, stride, size)
        stride *= size
    return total


def swap_tensor(values, n):
    return lax.ppermute(values, "tensor", [(t, t ^ 1) for t in range(n)])


def body(
    block_input,
    norm_gain,
    z_weight,
    x_weight,
    bc_weight,
    dt_weight,
    x_conv,
    x_conv_bias,
    bc_conv,
    bc_conv_bias,
    dt_bias,
    a_log,
    d_skip,
    gated_gain,
    out_weight,
    out_cotangent,
):
    n_dp, n_tensor = lax.axis_size("dp"), lax.axis_size("tensor")
    rows, model = block_input.shape
    inner = x_weight.shape[1]
    head_count = dt_weight.shape[1]
    head_dim = inner // head_count
    states = bc_weight.shape[1] // 2
    taps = x_conv.shape[0]
    heads = 4
    width = heads * head_dim
    blocks = inner // width
    chunks = rows // SPAN
    per_seq = LEN // SPAN
    inner_total = inner * n_tensor
    lanes = 128

    def tripled(v):
        one = jnp.pad(v, ((0, 0), (0, GROUP - head_count)))
        return jnp.pad(jnp.concatenate((one, one, one), axis=1), ((0, 0), (0, lanes - 3 * GROUP)))

    dt_w = tripled(dt_weight)
    dt_b = tripled(dt_bias[None])
    a_l = tripled(a_log[None])
    skip = jnp.repeat(d_skip, head_dim)[None]
    gain_in = norm_gain[None]
    gain_gated = gated_gain[None]
    x_bias = x_conv_bias[None]
    bc_bias = bc_conv_bias[None]

    def whole(array):
        return (array, array.shape, lambda j: (0,) * array.ndim)

    def columns(array):
        return (array, (array.shape[0], width), lambda j: (0, j))

    shared = Named(
        norm_gain=whole(gain_in),
        x_w=columns(x_weight),
        z_w=columns(z_weight),
        bc_w=whole(bc_weight),
        dt_w=whole(dt_w),
        x_conv=columns(x_conv),
        x_conv_bias=columns(x_bias),
        bc_conv=whole(bc_conv),
        bc_conv_bias=whole(bc_bias),
        dt_bias=whole(dt_b),
        a_log=whole(a_l),
        d_skip=columns(skip),
        gated_gain=columns(gain_gated),
    )

    kept = Named()
    shares = []
    states_at = []
    x_halo = bc_halo = None
    for i in range(chunks):
        first = i % per_seq == 0

        def at_rows(j, i=i):
            return (i, 0)

        def at_block(j, i=i):
            return (i, j)

        operands = Named(shared)
        operands.xin = (block_input, (SPAN, model), at_rows)
        operands.cot = (out_cotangent, (SPAN, model), at_rows)
        operands.out_w = (out_weight, (width, model), lambda j: (j, 0))
        if not first:
            operands.x_halo = columns(x_halo)
            operands.bc_halo = whole(bc_halo)
            operands.state = columns(states_at[-1])
        outs = Named(
            u_out=(shape(SPAN, model), (SPAN, model), lambda j: (0, 0)),
            state_out=(shape(states, inner), (states, width), lambda j: (0, j)),
            x_halo_out=(shape(HALO, inner), (HALO, width), lambda j: (0, j)),
            bc_halo_out=(shape(HALO, 2 * states), (HALO, 2 * states), lambda j: (0, 0)),
            sums=(shape(HALO, rows), (HALO, SPAN), lambda j, i=i: (0, i)),
            normed=(shape(rows, model, kind=BF16), (SPAN, model), at_rows),
            bc_pre=(shape(rows, 2 * states), (SPAN, 2 * states), at_rows),
            dt_pre=(shape(rows, lanes), (SPAN, lanes), at_rows),
            x_pre=(shape(rows, inner), (SPAN, width), at_block),
            z_pre=(shape(rows, inner), (SPAN, width), at_block),
            mg=(shape(rows, inner), (SPAN, width), at_block),
            y=(shape(rows, inner), (SPAN, width), at_block),
            gb=(shape(rows, inner, kind=BF16), (SPAN, width), at_block),
        )
        scratch = Named(
            bc_buf=((SPAN + HALO, 2 * states), F32),
            x_buf=((SPAN + HALO, width), F32),
            cb=((SPAN, 2 * states), BF16),
            bt=((2 * states, SPAN), BF16),
            scores=((SPAN, SPAN), F32),
            cum_t=((lanes, SPAN), F32),
            parts=((2 * SPAN, lanes), BF16),
            acc=((2 * SPAN, width), F32),
        )
        given = run_kernel(
            functools.partial(fwd_kernel, first, heads, head_dim),
            blocks,
            operands,
            outs,
            scratch,
            kept,
            flops=2 * SPAN * model * inner * 5,
            moved=2 * 3 * model * inner + 24 * SPAN * inner,
        )
        shares.append(given.pop("u_out"))
        states_at.append(given.pop("state_out"))
        x_halo = given.pop("x_halo_out")
        bc_halo = given.pop("bc_halo_out")
        kept = given

    sums = kept.sums
    sums_other = swap_tensor(sums, n_tensor)
    shares_other = [swap_tensor(u, n_tensor) for u in shares]

    square_sum = sums[0] + sums_other[0]
    gate_rms = lax.rsqrt(square_sum / inner_total + EPS)

    cot_scaled = (out_cotangent.astype(F32) * gate_rms[:, None]).astype(BF16)
    out_part = scattered_product(by_stage(cot_scaled.T, n_dp), kept.gb, n_dp)

    lows = Named()
    carry = Named()
    in_parts = [None] * chunks
    for i in reversed(range(chunks)):
        first = i % per_seq == 0
        last_chunk = i % per_seq == per_seq - 1
        start = i == chunks - 1

        def at_rows(j, i=i):
            return (i, 0)

        def at_block(j, i=i):
            return (i, j)

        operands = Named(shared)
        operands.xin = (block_input, (SPAN, model), at_rows)
        for name in ("bc_pre", "dt_pre"):
            operands[name] = (kept[name], (SPAN, kept[name].shape[1]), at_rows)
        for name in ("x_pre", "z_pre", "mg", "y"):
            operands[name] = (kept[name], (SPAN, width), at_block)
        operands.sums = (sums, (HALO, SPAN), lambda j, i=i: (0, i))
        operands.sums_other = (sums_other, (HALO, SPAN), lambda j, i=i: (0, i))
        before = i * (SPAN // HALO) - 1
        if not first:
            operands.x_halo = (kept.x_pre, (HALO, width), lambda j, b=before: (b, j))
            operands.bc_halo = (kept.bc_pre, (HALO, 2 * states), lambda j, b=before: (b, 0))
            operands.state = columns(states_at[i - 1])
        if not last_chunk:
            operands.d_state = columns(carry.d_state_out)
            operands.du_halo = columns(carry.du_halo_out)
            operands.du_bc_halo = whole(carry.du_bc_halo_out)
            operands.x_sums_in = columns(carry.x_sums)
            for name in ("head_sums", "bc_sums", "gain_sums"):
                operands[name + "_in"] = whole(carry[name])
        outs = Named(
            in_part=(shape(SPAN, model), (SPAN, model), lambda j: (0, 0)),
            du_halo_out=(shape(HALO, inner), (HALO, width), lambda j: (0, j)),
            du_bc_halo_out=(shape(HALO, 2 * states), (HALO, 2 * states), lambda j: (0, 0)),
            x_sums=(shape(HALO, inner), (HALO, width), lambda j: (0, j)),
            head_sums=(shape(HALO, lanes), (HALO, lanes), lambda j: (0, 0)),
            bc_sums=(shape(HALO, 2 * states), (HALO, 2 * states), lambda j: (0, 0)),
            gain_sums=(shape(HALO, model), (HALO, model), lambda j: (0, 0)),
            z_low=(shape(rows, inner, kind=BF16), (SPAN, width), at_block),
            x_low=(shape(rows, inner, kind=BF16), (SPAN, width), at_block),
            bc_low=(shape(rows, 2 * states, kind=BF16), (SPAN, 2 * states), at_rows),
            dt_low=(shape(rows, lanes, kind=BF16), (SPAN, lanes), at_rows),
        )
        if not first:
            outs.d_state_out = (shape(states, inner), (states, width), lambda j: (0, j))
        scratch = Named(
            bc_buf=((SPAN + HALO, 2 * states), F32),
            x_buf=((SPAN + HALO, width), F32),
            bc_grad_buf=((SPAN + HALO, 2 * states), F32),
            x_grad_buf=((SPAN + HALO, width), F32),
            bc_slope=((SPAN, 2 * states), F32),
            bb=((SPAN, 2 * states), BF16),
            cb=((SPAN, 2 * states), BF16),
            ct=((2 * states, SPAN), BF16),
            scores=((SPAN, SPAN), F32),
            d_scores=((SPAN, SPAN), F32),
            dt=((SPAN, lanes), F32),
            cum_t=((lanes, SPAN), F32),
            parts=((2 * SPAN, lanes), BF16),
            db=((SPAN, states), F32),
            dc=((SPAN, states), F32),
            d_cum=((SPAN, lanes), F32),
            d_dt=((SPAN, lanes), F32),
            ng=((SPAN, model), F32),
            rows=((SPAN, lanes), F32),
        )
        given = run_kernel(
            functools.partial(bwd_kernel, first, last_chunk, heads, head_dim, inner_total),
            blocks,
            operands,
            outs,
            scratch,
            lows,
            flops=2 * SPAN * model * inner * 6,
            moved=2 * 2 * model * inner + 24 * SPAN * inner,
        )
        lows = Named(
            z_low=given.z_low, x_low=given.x_low, bc_low=given.bc_low, dt_low=given.dt_low
        )
        in_parts[i] = given.in_part
        if last_chunk and not start:
            for name in ("x_sums", "head_sums", "bc_sums", "gain_sums"):
                given[name] = given[name] + carry[name]
        carry = given

    shared_sums = jnp.concatenate(
        (carry.gain_sums[0], carry.bc_sums[: taps + 1].reshape(-1))
    )
    shared_sums = shared_sums + swap_tensor(shared_sums, n_tensor)
    in_other = [None] * chunks
    for i in reversed(range(chunks)):
        in_other[i] = swap_tensor(in_parts[i], n_tensor)

    by_head = carry.head_sums[:2, :head_count].reshape(-1)
    small = jnp.concatenate((carry.x_sums[: taps + 3].reshape(-1), by_head, shared_sums))
    length = small.shape[0]
    padded = -(-length // 1024) * 1024
    small = doubling_sum(jnp.pad(small, (0, padded - length)).reshape(8, -1), n_dp).reshape(-1)
    x_end = (taps + 3) * inner
    x_sums = small[:x_end].reshape(taps + 3, inner)
    gated_gain_grad = x_sums[0]
    d_skip_grad = x_sums[1].reshape(head_count, head_dim).sum(axis=1)
    x_conv_grad = x_sums[2 : taps + 2]
    x_conv_bias_grad = x_sums[taps + 2]
    dt_bias_grad = small[x_end : x_end + head_count]
    a_log_grad = small[x_end + head_count : x_end + 2 * head_count]
    gain_at = x_end + 2 * head_count
    bc_at = gain_at + model
    gain_total = small[gain_at:bc_at]
    bc_total = small[bc_at : bc_at + (taps + 1) * 2 * states].reshape(taps + 1, 2 * states)
    place = lax.axis_index("dp") * n_tensor + lax.axis_index("tensor")
    places = n_dp * n_tensor

    def own(values, axis):
        size = values.shape[axis] // places
        return lax.dynamic_slice_in_dim(values, place * size, size, axis)

    norm_gain_grad = own(gain_total, 0)
    bc_conv_grad = own(bc_total[:taps], 1)
    bc_conv_bias_grad = own(bc_total[taps], 0)

    normed_rows = by_stage(kept.normed.T, n_dp)
    z_side = jnp.concatenate((lows.z_low, lows.bc_low, lows.dt_low), axis=1)
    z_part = scattered_product(normed_rows, z_side, n_dp)
    x_weight_grad = scattered_product(normed_rows, lows.x_low, n_dp)
    z_weight_grad = z_part[:, :inner]
    bc_part = z_part[:, inner : inner + 2 * states]
    dt_weight_grad = z_part[:, inner + 2 * states : inner + 2 * states + head_count]
    bc_part = bc_part.reshape(n_tensor, -1, 2 * states)
    mine = lax.axis_index("tensor")
    bc_weight_grad = lax.dynamic_index_in_dim(bc_part, mine, 0, keepdims=False) + swap_tensor(
        lax.dynamic_index_in_dim(bc_part, 1 - mine, 0, keepdims=False), n_tensor
    )
    out_weight_grad = out_part.T

    block_output = jnp.zeros((rows, model), BF16)
    for i in range(chunks):
        at = slice(i * SPAN, (i + 1) * SPAN)
        total = (shares[i] + shares_other[i]) * gate_rms[at, None]
        block_output = block_output.at[at].set((block_input[at].astype(F32) + total).astype(BF16))
    input_grad = jnp.zeros((rows, model), BF16)
    for i in reversed(range(chunks)):
        at = slice(i * SPAN, (i + 1) * SPAN)
        total = out_cotangent[at].astype(F32) + (in_parts[i] + in_other[i])
        input_grad = input_grad.at[at].set(total.astype(BF16))
    return (
        block_output,
        input_grad,
        norm_gain_grad,
        z_weight_grad,
        x_weight_grad,
        bc_weight_grad,
        dt_weight_grad,
        x_conv_grad,
        x_conv_bias_grad,
        bc_conv_grad,
        bc_conv_bias_grad,
        dt_bias_grad,
        a_log_grad,
        d_skip_grad,
        gated_gain_grad,
        out_weight_grad,
    )


def solution(mesh):
    in_specs = (
        P("dp", None),
        P(),
        P(None, "tensor"),
        P(None, "tensor"),
        P(),
        P(None, "tensor"),
        P(None, "tensor"),
        P("tensor"),
        P(),
        P(),
        P("tensor"),
        P("tensor"),
        P("tensor"),
        P("tensor"),
        P("tensor", None),
        P("dp", None),
    )
    out_specs = (
        P("dp", None),
        P("dp", None),
        P(("dp", "tensor")),
        P("dp", "tensor"),
        P("dp", "tensor"),
        P(("dp", "tensor"), None),
        P("dp", "tensor"),
        P(None, "tensor"),
        P("tensor"),
        P(None, ("dp", "tensor")),
        P(("dp", "tensor")),
        P("tensor"),
        P("tensor"),
        P("tensor"),
        P("tensor"),
        P("tensor", "dp"),
    )
    return jax.shard_map(body, mesh=mesh, in_specs=in_specs, out_specs=out_specs, check_vma=False)
```

time: 1230 us -> 632 us (0.51)
  matrix products: 325 us -> 30.6 us
  other arithmetic: 264 us -> 22.4 us
  Pallas kernels: 0 us -> 169 us
  blocking collectives: 98.2 us -> 0 us
  waiting for transfers between devices: 366 us -> 296 us
  local copies, waits for them, and re-layouts: 111 us -> 50.4 us
  starting transfers between devices: 0.25 us -> 51.7 us
  loops' own time: 33.9 us -> 0 us
  between operations: 16.5 us -> 1.8 us
    ppermute x0 -> x39, waiting for transfers between devices: none -> 296 us  [the longest x11 136 us: swap_tensor(): return lax.ppermute(values, 'tensor', [(t, t ^ 1) for t in range(n)])]
    dot_general x54 -> x6, matrix products: 321 us -> 30.6 us  [share(): return jnp.dot(mine, right, preferred_element_type=F32)]
    reduce_scatter x4 -> x0, waiting for transfers between devices: 200 us -> none  [the longest x1 116 us: body(): lax.psum_scatter(z_weight_part, 'dp', scatter_dimension=0, tiled=True)]
    pallas_call x0 -> x8, Pallas kernels: none -> 169 us  [run_kernel(): pl.pallas_call(kernel, grid=(grid,), in_specs=specs, out_specs=[pl.BlockS...]
    psum x1 -> x0, waiting for transfers between devices: 166 us -> none  [body(): lax.psum(partial_out, 'tensor')]
    psum x3 -> x0, blocking collectives: 56.9 us -> none  [the longest x1 47 us: body(): lax.psum((conv_grads[2], conv_grads[3], dt_bias_part, a_log_part, d_skip_...]
    mul x36 -> x0, other arithmetic: 54.2 us -> none  [the longest x9 24.8 us: scan_heads(): inputs_x * steps_dt[..., None]]
    ppermute x0 -> x39, starting transfers between devices: none -> 51.7 us  [the longest x9 22.6 us: line_sum(): lax.ppermute(send, 'dp', hops(n, stride, size, 1, lambda p: p <= step - 1))]
  transfers between devices with their start and end apart: 6 -> 39, of which waited for: 3 -> 17; matrix products, arithmetic and copies ran while one was open for 10% -> 14% of each run, Pallas kernels for 0% -> 15%
where the time goes in v1:
time: 632 us; the launch traced here: 621 us
  waiting for transfers between devices  296 us (47%)
  Pallas kernels  169 us (27%)
  starting transfers between devices  51.7 us (8%)
  local copies, waits for them, and re-layouts  50.4 us (8%)
  matrix products  30.6 us (5%)
  other arithmetic  22.4 us (4%)
    pallas_call x8, Pallas kernels, run_kernel(): pl.pallas_call(kernel, grid=(grid,), in_specs=specs, out_specs=[pl.BlockS...  169 us
    ppermute x11, waiting for transfers between devices, swap_tensor(): return lax.ppermute(values, 'tensor', [(t, t ^ 1) for t in range(n)])  136 us
    ppermute x3, waiting for transfers between devices, line_sum(): lax.ppermute(block(1 - place), 'dp', hops(n, stride, size, 1, lambda p: T...  62.6 us
    ppermute x9, waiting for transfers between devices, line_sum(): lax.ppermute(send, 'dp', hops(n, stride, size, 1, lambda p: p <= step - 1))  62.6 us
    ppermute x9, waiting for transfers between devices, line_sum(): lax.ppermute(send, 'dp', hops(n, stride, size, -1, lambda p: p >= size -...  31.7 us
    dot_general x6, matrix products, share(): return jnp.dot(mine, right, preferred_element_type=F32)  30.6 us
    ppermute x9, starting transfers between devices, line_sum(): lax.ppermute(send, 'dp', hops(n, stride, size, 1, lambda p: p <= step - 1))  22.6 us
    unnamed x51, local copies, waits for them, and re-layouts  18.5 us
  transfers between devices with their start and end apart: 39, of which 17 were waited for; matrix products, arithmetic and copies ran while one was open for 14% of the time, Pallas kernels for 15%

profile of v1, /device:TPU:14, one launch (start us, length us, event | category | flops | bytes accessed | tf_op | source)
XLA Modules:
  0.0 621.4 jit_solution(10513094397634451687)
XLA Ops:
  10.2 20.1 %shard_map.279 = (f32[256,1536]{1,0:T(8,128)}, f32[128,1536]{1,0:T(8,128)}, f32[8,1536]{1,0:T(8,128)}, f32[8,256]{1,0:T(8,128)}, f32[8,1024]{1,0:T(8,128)}, /*in...) custom-call(f32[1,1536]{1,0:T(1,128)} %broadcast_in_dim.26.refs_0_, ...), custom_call_target="tpu_custom_call" | custom-call | flops 6039797760 | bytes 23592960 | tf_op jit(solution)/shard_map/pallas_call | solution.py:454
  30.2 19.2 %shard_map.280 = (f32[256,1536]{1,0:T(8,128)}, f32[128,1536]{1,0:T(8,128)}, f32[8,1536]{1,0:T(8,128)}, f32[8,256]{1,0:T(8,128)}, f32[8,1024]{1,0:T(8,128)}, /*in...) custom-call(f32[1,1536]{1,0:T(1,128)} %broadcast_in_dim.26.refs_0_, ...), custom_call_target="tpu_custom_call", output_to_operand_aliasing={{4}: (19, {}), {5}: (20, {}), {6}: (21, {}), {7}: (22, {}),... | custom-call | flops 6039797760 | bytes 23592960 | tf_op jit(solution)/shard_map/pallas_call | solution.py:454
  49.4 19.2 %shard_map.281 = (f32[256,1536]{1,0:T(8,128)}, f32[128,1536]{1,0:T(8,128)}, f32[8,1536]{1,0:T(8,128)}, f32[8,256]{1,0:T(8,128)}, f32[8,1024]{1,0:T(8,128)}, /*in...) custom-call(f32[1,1536]{1,0:T(1,128)} %broadcast_in_dim.26.refs_0_, ...), custom_call_target="tpu_custom_call", output_to_operand_aliasing={{4}: (19, {}), {5}: (20, {}), {6}: (21, {}), {7}: (22, {}),... | custom-call | flops 6039797760 | bytes 23592960 | tf_op jit(solution)/shard_map/pallas_call | solution.py:454
  68.7 19.4 %shard_map.282 = (f32[256,1536]{1,0:T(8,128)}, f32[128,1536]{1,0:T(8,128)}, f32[8,1536]{1,0:T(8,128)}, f32[8,256]{1,0:T(8,128)}, f32[8,1024]{1,0:T(8,128)}, /*in...) custom-call(f32[1,1536]{1,0:T(1,128)} %broadcast_in_dim.26.refs_0_, ...), custom_call_target="tpu_custom_call", output_to_operand_aliasing={{4}: (19, {}), {5}: (20, {}), {6}: (21, {}), {7}: (22, {}),... | custom-call | flops 6039797760 | bytes 23592960 | tf_op jit(solution)/shard_map/pallas_call | solution.py:454
  92.2 4.6 copy.76
  96.9 4.2 dynamic-slice_bitcast_fusion.6
  101.1 2.8 copy.79
  103.9 2.8 copy.78
  113.3 4.3 fusion.20
  117.6 21.4 %shard_map.283 = (f32[256,1536]{1,0:T(8,128)}, f32[8,1536]{1,0:T(8,128)}, f32[8,256]{1,0:T(8,128)}, f32[8,1536]{1,0:T(8,128)}, f32[8,128]{1,0:T(8,128)}, /*index...) custom-call(f32[1,1536]{1,0:T(1,128)} %broadcast_in_dim.26.refs_0_, ...), custom_call_target="tpu_custom_call" | custom-call | flops 7247757312 | bytes 18874368 | tf_op jit(solution)/shard_map/pallas_call | solution.py:454
  139.0 23.2 %shard_map.284 = (f32[256,1536]{1,0:T(8,128)}, f32[8,1536]{1,0:T(8,128)}, f32[8,256]{1,0:T(8,128)}, f32[8,1536]{1,0:T(8,128)}, f32[8,128]{1,0:T(8,128)}, /*index...) custom-call(f32[1,1536]{1,0:T(1,128)} %broadcast_in_dim.26.refs_0_, ...), custom_call_target="tpu_custom_call", output_to_operand_aliasing={{7}: (32, {}), {8}: (33, {}), {9}: (34, {}), {10}: (35, {})} | custom-call | flops 7247757312 | bytes 18874368 | tf_op jit(solution)/shard_map/pallas_call | solution.py:454
  162.2 23.4 %shard_map.285 = (f32[256,1536]{1,0:T(8,128)}, f32[8,1536]{1,0:T(8,128)}, f32[8,256]{1,0:T(8,128)}, f32[8,1536]{1,0:T(8,128)}, f32[8,128]{1,0:T(8,128)}, /*index...) custom-call(f32[1,1536]{1,0:T(1,128)} %broadcast_in_dim.26.refs_0_, ...), custom_call_target="tpu_custom_call", output_to_operand_aliasing={{7}: (32, {}), {8}: (33, {}), {9}: (34, {}), {10}: (35, {})} | custom-call | flops 7247757312 | bytes 18874368 | tf_op jit(solution)/shard_map/pallas_call | solution.py:454
  185.7 22.6 %shard_map.286 = (f32[256,1536]{1,0:T(8,128)}, f32[8,1536]{1,0:T(8,128)}, f32[8,256]{1,0:T(8,128)}, f32[8,1536]{1,0:T(8,128)}, f32[8,128]{1,0:T(8,128)}, /*index...) custom-call(f32[1,1536]{1,0:T(1,128)} %broadcast_in_dim.26.refs_0_, ...), custom_call_target="tpu_custom_call", output_to_operand_aliasing={{7}: (29, {}), {8}: (30, {}), {9}: (31, {}), {10}: (32, {})} | custom-call | flops 7247757312 | bytes 18874368 | tf_op jit(solution)/shard_map/pallas_call | solution.py:454
  210.4 4.0 constant_dynamic-update-slice_fusion.2
  218.0 2.9 collective-permute-done.11
  221.4 7.6 %fusion.18 = f32[768,1920]{1,0:T(8,128)} fusion(bf16[768,1024]{1,0:T(8,128)(2,1)S(1)} %bitcast.123, bf16[1024,1920]{1,0:T(8,128)(2,1)} %constant_dynamic-update-slice_fusion), kind=kOutput, calls=%fused_computation.79 | convolution fusion | flops 3019898880 | bytes 11403264 | tf_op jit(solution)/shard_map/dot_general | solution.py:553
  229.0 2.6 collective-permute-start.13
  231.7 4.3 fusion.19
  243.9 2.2 add_convert_fusion.7
  248.0 2.2 fusion
  250.2 2.3 fusion.1
  252.5 27.4 %collective-permute-done.4 = f32[256,1536]{1,0:T(8,128)S(1)} collective-permute-done((f32[256,1536]{1,0:T(8,128)}, f32[256,1536]{1,0:T(8,128)S(1)}, u32[]{:S(2)}, u32[]{:S(2)}) %collective-permute-start.4) | collective-permute-done | bytes 1572896 | tf_op jit(solution)/shard_map/ppermute | solution.py:566
  281.8 31.8 %collective-permute-done.5 = f32[256,1536]{1,0:T(8,128)S(1)} collective-permute-done((f32[256,1536]{1,0:T(8,128)S(1)}, f32[256,1536]{1,0:T(8,128)S(1)}, u32[]{:S(2)}, u32[]{:S(2)}) %collective-permute-start.5) | collective-permute-done | bytes 1572896 | tf_op jit(solution)/shard_map/ppermute | solution.py:566
  318.0 4.5 convolution_add_fusion
  324.9 4.5 convolution_add_fusion.1
  331.5 5.5 convolution_add_fusion.2
  337.2 76.7 %collective-permute-done.6 = f32[256,1536]{1,0:T(8,128)} collective-permute-done((f32[256,1536]{1,0:T(8,128)S(1)}, f32[256,1536]{1,0:T(8,128)}, u32[]{:S(2)}, u32[]{:S(2)}) %collective-permute-start.6) | collective-permute-done | bytes 1572896 | tf_op jit(solution)/shard_map/ppermute | solution.py:566
  416.2 2.2 fusion.4
  418.5 2.2 fusion.5
  424.7 2.8 collective-permute-done.23
  427.9 59.8 %collective-permute-done.15 = f32[4,96,1920]{2,1,0:T(8,128)S(1)} collective-permute-done((f32[4,96,1920]{2,1,0:T(8,128)S(1)}, f32[4,96,1920]{2,1,0:T(8,128)S(1)}, u32[]{:S(2)}, u32[]{:S(2)}) %collective-permute-start.15) | collective-permute-done | bytes 2949152 | tf_op jit(solution)/shard_map/ppermute | solution.py:502
  491.7 1.9 collective-permute-start.34
  493.6 15.9 %collective-permute-done.16 = f32[96,1920]{1,0:T(8,128)S(1)} collective-permute-done((f32[96,1920]{1,0:T(8,128)S(1)}, f32[96,1920]{1,0:T(8,128)S(1)}, u32[]{:S(2)}, u32[]{:S(2)}) %collective-permute-start.16) | collective-permute-done | bytes 737312 | tf_op jit(solution)/shard_map/ppermute | solution.py:511
  510.3 11.8 %collective-permute-done.24 = f32[96,1536]{1,0:T(8,128)S(1)} collective-permute-done((f32[96,1536]{1,0:T(8,128)S(1)}, f32[96,1536]{1,0:T(8,128)S(1)}, u32[]{:S(2)}, u32[]{:S(2)}) %collective-permute-start.24) | collective-permute-done | bytes 589856 | tf_op jit(solution)/shard_map/ppermute | solution.py:511
  524.1 1.9 collective-permute-start.25
  526.1 8.7 %collective-permute-done.34 = f32[96,1536]{1,0:T(8,128)S(1)} collective-permute-done((f32[96,1536]{1,0:T(8,128)S(1)}, f32[96,1536]{1,0:T(8,128)S(1)}, u32[]{:S(2)}, u32[]{:S(2)}) %collective-permute-start.34) | collective-permute-done | bytes 589856 | tf_op jit(solution)/shard_map/ppermute | solution.py:511
  536.3 4.6 collective-permute-start.35
  540.8 9.8 %collective-permute-done.17 = f32[96,1920]{1,0:T(8,128)S(1)} collective-permute-done((f32[96,1920]{1,0:T(8,128)S(1)}, f32[96,1920]{1,0:T(8,128)S(1)}, u32[]{:S(2)}, u32[]{:S(2)}) %collective-permute-start.17) | collective-permute-done | bytes 737312 | tf_op jit(solution)/shard_map/ppermute | solution.py:511
  552.1 11.1 %collective-permute-done.25 = f32[96,1536]{1,0:T(8,128)S(1)} collective-permute-done((f32[96,1536]{1,0:T(8,128)S(1)}, f32[96,1536]{1,0:T(8,128)S(1)}, u32[]{:S(2)}, u32[]{:S(2)}) %collective-permute-start.25) | collective-permute-done | bytes 589856 | tf_op jit(solution)/shard_map/ppermute | solution.py:511
  564.7 4.6 collective-permute-start.26
  569.3 1.9 collective-permute-start.38
  571.3 3.9 collective-permute-start.18
  575.3 6.2 %collective-permute-done.28 = f32[96,1536]{1,0:T(8,128)S(1)} collective-permute-done((f32[96,1536]{1,0:T(8,128)S(1)}, f32[96,1536]{1,0:T(8,128)S(1)}, u32[]{:S(2)}, u32[]{:S(2)}) %collective-permute-start.28) | collective-permute-done | bytes 589856 | tf_op jit(solution)/shard_map/ppermute | solution.py:514
  583.6 1.9 collective-permute-start.29
  585.5 8.7 %collective-permute-done.38 = f32[96,1536]{1,0:T(8,128)S(1)} collective-permute-done((f32[96,1536]{1,0:T(8,128)S(1)}, f32[96,1536]{1,0:T(8,128)S(1)}, u32[]{:S(2)}, u32[]{:S(2)}) %collective-permute-start.38) | collective-permute-done | bytes 589856 | tf_op jit(solution)/shard_map/ppermute | solution.py:514
  595.1 5.3 collective-permute-done.18
  600.4 9.6 %collective-permute-done.21 = f32[96,1920]{1,0:T(8,128)S(1)} collective-permute-done((f32[96,1920]{1,0:T(8,128)S(1)}, f32[96,1920]{1,0:T(8,128)S(1)}, u32[]{:S(2)}, u32[]{:S(2)}) %collective-permute-start.21) | collective-permute-done | bytes 737312 | tf_op jit(solution)/shard_map/ppermute | solution.py:514
  610.7 7.2 %collective-permute-done.29 = f32[96,1536]{1,0:T(8,128)S(1)} collective-permute-done((f32[96,1536]{1,0:T(8,128)S(1)}, f32[96,1536]{1,0:T(8,128)S(1)}, u32[]{:S(2)}, u32[]{:S(2)}) %collective-permute-start.29) | collective-permute-done | bytes 589856 | tf_op jit(solution)/shard_map/ppermute | solution.py:514
  (180 shorter events, 71.7 us)
Async XLA Ops:
  88.1 20.0 %collective-permute-start.1 = (f32[8,1024]{1,0:T(8,128)}, f32[8,1024]{1,0:T(8,128)S(1)}, u32[]{:S(2)}, u32[]{:S(2)}) collective-permute-start(f32[8,1024]{1,0:T(8,128)} %get-tuple-element.243.refs_20_), channel_id=1, source_target_pairs={{0,1},{1,0},{2,3},{3,2},{4,5},{5,4},{6,7},{7,6},{8,9},{9,8},{10,11... | collective-permute-start | bytes 98312 | tf_op jit(solution)/shard_map/ppermute | solution.py:566
  88.7 148.6 %collective-permute-start = (f32[256,1536]{1,0:T(8,128)}, f32[256,1536]{1,0:T(8,128)}, u32[]{:S(2)}, u32[]{:S(2)}) collective-permute-start(f32[256,1536]{1,0:T(8,128)} %get-tuple-element.206), channel_id=1, source_target_pairs={{0,1},{1,0},{2,3},{3,2},{4,5},{5,4},{6,7},{7,6},{8,9},{9,8},{10,11... | collective-permute-start | bytes 4718600 | tf_op jit(solution)/shard_map/ppermute | solution.py:566
  90.2 152.2 %collective-permute-start.2 = (f32[256,1536]{1,0:T(8,128)}, f32[256,1536]{1,0:T(8,128)}, u32[]{:S(2)}, u32[]{:S(2)}) collective-permute-start(f32[256,1536]{1,0:T(8,128)} %get-tuple-element.244), channel_id=1, source_target_pairs={{0,1},{1,0},{2,3},{3,2},{4,5},{5,4},{6,7},{7,6},{8,9},{9,8},{10,11... | collective-permute-start | bytes 4718600 | tf_op jit(solution)/shard_map/ppermute | solution.py:566
  90.7 155.6 %collective-permute-start.3 = (f32[256,1536]{1,0:T(8,128)}, f32[256,1536]{1,0:T(8,128)}, u32[]{:S(2)}, u32[]{:S(2)}) collective-permute-start(f32[256,1536]{1,0:T(8,128)} %get-tuple-element.245), channel_id=1, source_target_pairs={{0,1},{1,0},{2,3},{3,2},{4,5},{5,4},{6,7},{7,6},{8,9},{9,8},{10,11... | collective-permute-start | bytes 4718600 | tf_op jit(solution)/shard_map/ppermute | solution.py:566
  103.9 5.0 copy-start.7
  117.6 198.1 %collective-permute-start.31 = (f32[768,1536]{1,0:T(8,128)}, f32[768,1536]{1,0:T(8,128)}, u32[]{:S(2)}, u32[]{:S(2)}) collective-permute-start(f32[768,1536]{1,0:T(8,128)} %fusion.20), channel_id=1, source_target_pairs={{0,2},{2,0},{4,6},{6,4},{8,10},{10,8},{12,14},{14,12},{16,18},{18,... | collective-permute-start | bytes 14155784 | tf_op jit(solution)/shard_map/ppermute | solution.py:555
  209.8 5.4 collective-permute-start.9
  210.4 5.2 copy-start.8
  210.4 6.8 %copy-start.11 = (bf16[1024,128]{1,0:T(8,128)(2,1)S(1)}, bf16[1024,128]{1,0:T(8,128)(2,1)}, u32[]{:S(2)}) copy-start(bf16[1024,128]{1,0:T(8,128)(2,1)} %get-tuple-element.297) | copy-start | bytes 786436
  210.4 11.0 %copy-start.17 = (bf16[1,2,4,96,1024]{4,3,2,1,0:T(8,128)(2,1)S(1)}, bf16[1,2,4,96,1024]{4,3,2,1,0:T(8,128)(2,1)}, u32[]{:S(2)}) copy-start(bf16[1,2,4,96,1024]{4,3,2,1,0:T(8,128)(2,1)} %copy.78) | copy-start | bytes 4718596
  215.3 1.3 collective-permute-start.10
  216.6 4.2 collective-permute-start.11
  220.9 8.2 %collective-permute-start.12 = (f32[8,1792]{1,0:T(8,128)S(1)}, f32[8,1792]{1,0:T(8,128)S(1)}, u32[]{:S(2)}, u32[]{:S(2)}) collective-permute-start(f32[8,1792]{1,0:T(8,128)S(1)} %add.324), channel_id=1, source_target_pairs={{0,8},{2,10},{4,12},{6,14},{8,0},{10,2},{12,4},{14,6},{16,24},{18,... | collective-permute-start | bytes 172040 | tf_op jit(solution)/shard_map/ppermute | solution.py:523
  221.4 10.3 %copy-start.3 = (bf16[1024,1536]{1,0:T(8,128)(2,1)S(1)}, bf16[1024,1536]{1,0:T(8,128)(2,1)}, u32[]{:S(2)}) copy-start(bf16[1024,1536]{1,0:T(8,128)(2,1)} %get-tuple-element.298) | copy-start | bytes 9437188
  229.0 8.2 %collective-permute-start.13 = (f32[8,1792]{1,0:T(8,128)S(1)}, f32[8,1792]{1,0:T(8,128)S(1)}, u32[]{:S(2)}, u32[]{:S(2)}) collective-permute-start(f32[8,1792]{1,0:T(8,128)S(1)} %add.325), channel_id=1, source_target_pairs={{0,16},{2,18},{4,20},{6,22},{8,24},{10,26},{12,28},{14,30},{16,0},... | collective-permute-start | bytes 172040 | tf_op jit(solution)/shard_map/ppermute | solution.py:523
  236.0 8.0 %copy-start = (bf16[1024,1536]{1,0:T(8,128)(2,1)S(1)}, bf16[1024,1536]{1,0:T(8,128)(2,1)}, u32[]{:S(2)}) copy-start(bf16[1024,1536]{1,0:T(8,128)(2,1)} %refs_13_.15) | copy-start | bytes 9437188
  237.2 92.3 %collective-permute-start.14 = (f32[768,1920]{1,0:T(8,128)}, f32[768,1920]{1,0:T(8,128)}, u32[]{:S(2)}, u32[]{:S(2)}) collective-permute-start(f32[768,1920]{1,0:T(8,128)} %fusion.18), channel_id=1, source_target_pairs={{0,2},{2,0},{4,6},{6,4},{8,10},{10,8},{12,14},{14,12},{16,18},{18,... | collective-permute-start | bytes 17694728 | tf_op jit(solution)/shard_map/ppermute | solution.py:555
  237.2 85.5 %collective-permute-start.22 = (f32[768,1536]{1,0:T(8,128)}, f32[768,1536]{1,0:T(8,128)}, u32[]{:S(2)}, u32[]{:S(2)}) collective-permute-start(f32[768,1536]{1,0:T(8,128)} %fusion.19), channel_id=1, source_target_pairs={{0,2},{2,0},{4,6},{6,4},{8,10},{10,8},{12,14},{14,12},{16,18},{18,... | collective-permute-start | bytes 14155784 | tf_op jit(solution)/shard_map/ppermute | solution.py:555
  242.4 37.5 %collective-permute-start.4 = (f32[256,1536]{1,0:T(8,128)}, f32[256,1536]{1,0:T(8,128)S(1)}, u32[]{:S(2)}, u32[]{:S(2)}) collective-permute-start(f32[256,1536]{1,0:T(8,128)} %get-tuple-element.246), channel_id=1, source_target_pairs={{0,1},{1,0},{2,3},{3,2},{4,5},{5,4},{6,7},{7,6},{8,9},{9,8},{10,11... | collective-permute-start | bytes 4718600 | tf_op jit(solution)/shard_map/ppermute | solution.py:566
  247.5 66.1 %collective-permute-start.5 = (f32[256,1536]{1,0:T(8,128)S(1)}, f32[256,1536]{1,0:T(8,128)S(1)}, u32[]{:S(2)}, u32[]{:S(2)}) collective-permute-start(f32[256,1536]{1,0:T(8,128)S(1)} %copy-done.20), channel_id=1, source_target_pairs={{0,1},{1,0},{2,3},{3,2},{4,5},{5,4},{6,7},{7,6},{8,9},{9,8},{10,11... | collective-permute-start | bytes 4718600 | tf_op jit(solution)/shard_map/ppermute | solution.py:566
  250.2 31.2 %copy-start.15 = (f32[256,1536]{1,0:T(8,128)S(1)}, f32[256,1536]{1,0:T(8,128)}, u32[]{:S(2)}) copy-start(f32[256,1536]{1,0:T(8,128)} %get-tuple-element.246) | copy-start | bytes 4718596
  252.5 62.6 %copy-start.2 = (bf16[1024,1536]{1,0:T(8,128)(2,1)S(1)}, bf16[1024,1536]{1,0:T(8,128)(2,1)}, u32[]{:S(2)}) copy-start(bf16[1024,1536]{1,0:T(8,128)(2,1)} %refs_14_.7) | copy-start | bytes 9437188
  279.8 138.6 %collective-permute-start.8 = (f32[256,1536]{1,0:T(8,128)}, f32[256,1536]{1,0:T(8,128)}, u32[]{:S(2)}, u32[]{:S(2)}) collective-permute-start(f32[256,1536]{1,0:T(8,128)} %get-tuple-element.289), channel_id=1, source_target_pairs={{0,1},{1,0},{2,3},{3,2},{4,5},{5,4},{6,7},{7,6},{8,9},{9,8},{10,11... | collective-permute-start | bytes 4718600 | tf_op jit(solution)/shard_map/ppermute | solution.py:566
  281.7 33.3 %copy-start.13 = (bf16[1024,1536]{1,0:T(8,128)(2,1)}, bf16[1024,1536]{1,0:T(8,128)(2,1)S(1)}, u32[]{:S(2)}) copy-start(bf16[1024,1536]{1,0:T(8,128)(2,1)S(1)} %fusion.2) | copy-start | bytes 9437188
  313.6 102.7 %collective-permute-start.7 = (f32[256,1536]{1,0:T(8,128)}, f32[256,1536]{1,0:T(8,128)}, u32[]{:S(2)}, u32[]{:S(2)}) collective-permute-start(f32[256,1536]{1,0:T(8,128)} %get-tuple-element.277), channel_id=1, source_target_pairs={{0,1},{1,0},{2,3},{3,2},{4,5},{5,4},{6,7},{7,6},{8,9},{9,8},{10,11... | collective-permute-start | bytes 4718600 | tf_op jit(solution)/shard_map/ppermute | solution.py:566
  316.5 97.4 %collective-permute-start.6 = (f32[256,1536]{1,0:T(8,128)S(1)}, f32[256,1536]{1,0:T(8,128)}, u32[]{:S(2)}, u32[]{:S(2)}) collective-permute-start(f32[256,1536]{1,0:T(8,128)S(1)} %copy-done.19), channel_id=1, source_target_pairs={{0,1},{1,0},{2,3},{3,2},{4,5},{5,4},{6,7},{7,6},{8,9},{9,8},{10,11... | collective-permute-start | bytes 4718600 | tf_op jit(solution)/shard_map/ppermute | solution.py:566
  322.7 98.0 %collective-permute-start.32 = (f32[4,96,1536]{2,1,0:T(8,128)S(1)}, f32[4,96,1536]{2,1,0:T(8,128)S(1)}, u32[]{:S(2)}, u32[]{:S(2)}) collective-permute-start(f32[4,96,1536]{2,1,0:T(8,128)S(1)} %dynamic-slice_bitcast_fusion.1), channel_id=1, source_target_pairs={{0,4},{2,6},{8,12},{10,14},{16,20},{18,22},{24,28},{26,30},{4,0},{... | collective-permute-start | bytes 7077896 | tf_op jit(solution)/shard_map/ppermute | solution.py:502
  329.6 98.0 %collective-permute-start.23 = (f32[4,96,1536]{2,1,0:T(8,128)S(1)}, f32[4,96,1536]{2,1,0:T(8,128)S(1)}, u32[]{:S(2)}, u32[]{:S(2)}) collective-permute-start(f32[4,96,1536]{2,1,0:T(8,128)S(1)} %dynamic-slice_bitcast_fusion.2), channel_id=1, source_target_pairs={{0,4},{2,6},{8,12},{10,14},{16,20},{18,22},{24,28},{26,30},{4,0},{... | collective-permute-start | bytes 7077896 | tf_op jit(solution)/shard_map/ppermute | solution.py:502
  413.9 73.9 %collective-permute-start.15 = (f32[4,96,1920]{2,1,0:T(8,128)S(1)}, f32[4,96,1920]{2,1,0:T(8,128)S(1)}, u32[]{:S(2)}, u32[]{:S(2)}) collective-permute-start(f32[4,96,1920]{2,1,0:T(8,128)S(1)} %dynamic-slice_bitcast_fusion), channel_id=1, source_target_pairs={{0,4},{2,6},{8,12},{10,14},{16,20},{18,22},{24,28},{26,30},{4,0},{... | collective-permute-start | bytes 8847368 | tf_op jit(solution)/shard_map/ppermute | solution.py:502
  422.5 69.1 %collective-permute-start.33 = (f32[96,1536]{1,0:T(8,128)S(1)}, f32[96,1536]{1,0:T(8,128)S(1)}, u32[]{:S(2)}, u32[]{:S(2)}) collective-permute-start(f32[96,1536]{1,0:T(8,128)S(1)} %get-tuple-element.345), channel_id=1, source_target_pairs={{0,8},{2,10},{4,12},{6,14},{1,9},{3,11},{5,13},{7,15}} | collective-permute-start | bytes 1769480 | tf_op jit(solution)/shard_map/ppermute | solution.py:511
  423.8 100.4 %collective-permute-start.36 = (f32[96,1536]{1,0:T(8,128)S(1)}, f32[96,1536]{1,0:T(8,128)S(1)}, u32[]{:S(2)}, u32[]{:S(2)}) collective-permute-start(f32[96,1536]{1,0:T(8,128)S(1)} %get-tuple-element.346), channel_id=1, source_target_pairs={{24,16},{26,18},{28,20},{30,22},{25,17},{27,19},{29,21},{31,23}} | collective-permute-start | bytes 1769480 | tf_op jit(solution)/shard_map/ppermute | solution.py:514
  488.2 21.3 %collective-permute-start.16 = (f32[96,1920]{1,0:T(8,128)S(1)}, f32[96,1920]{1,0:T(8,128)S(1)}, u32[]{:S(2)}, u32[]{:S(2)}) collective-permute-start(f32[96,1920]{1,0:T(8,128)S(1)} %get-tuple-element.341), channel_id=1, source_target_pairs={{0,8},{2,10},{4,12},{6,14},{1,9},{3,11},{5,13},{7,15}} | collective-permute-start | bytes 2211848 | tf_op jit(solution)/shard_map/ppermute | solution.py:511
  489.6 32.6 %collective-permute-start.24 = (f32[96,1536]{1,0:T(8,128)S(1)}, f32[96,1536]{1,0:T(8,128)S(1)}, u32[]{:S(2)}, u32[]{:S(2)}) collective-permute-start(f32[96,1536]{1,0:T(8,128)S(1)} %get-tuple-element.349), channel_id=1, source_target_pairs={{0,8},{2,10},{4,12},{6,14},{1,9},{3,11},{5,13},{7,15}} | collective-permute-start | bytes 1769480 | tf_op jit(solution)/shard_map/ppermute | solution.py:511
  490.9 61.2 %collective-permute-start.27 = (f32[96,1536]{1,0:T(8,128)S(1)}, f32[96,1536]{1,0:T(8,128)S(1)}, u32[]{:S(2)}, u32[]{:S(2)}) collective-permute-start(f32[96,1536]{1,0:T(8,128)S(1)} %get-tuple-element.350), channel_id=1, source_target_pairs={{24,16},{26,18},{28,20},{30,22},{25,17},{27,19},{29,21},{31,23}} | collective-permute-start | bytes 1769480 | tf_op jit(solution)/shard_map/ppermute | solution.py:514
  491.7 43.1 %collective-permute-start.34 = (f32[96,1536]{1,0:T(8,128)S(1)}, f32[96,1536]{1,0:T(8,128)S(1)}, u32[]{:S(2)}, u32[]{:S(2)}) collective-permute-start(f32[96,1536]{1,0:T(8,128)S(1)} %bitcast_add_fusion.10), channel_id=1, source_target_pairs={{0,8},{2,10},{4,12},{6,14},{8,16},{10,18},{12,20},{14,22},{1,9},{3... | collective-permute-start | bytes 1769480 | tf_op jit(solution)/shard_map/ppermute | solution.py:511
  509.5 26.7 %collective-permute-start.19 = (f32[96,1920]{1,0:T(8,128)S(1)}, f32[96,1920]{1,0:T(8,128)S(1)}, u32[]{:S(2)}, u32[]{:S(2)}) collective-permute-start(f32[96,1920]{1,0:T(8,128)S(1)} %get-tuple-element.342), channel_id=1, source_target_pairs={{24,16},{26,18},{28,20},{30,22},{25,17},{27,19},{29,21},{31,23}} | collective-permute-start | bytes 2211848 | tf_op jit(solution)/shard_map/ppermute | solution.py:514
  522.1 28.4 %collective-permute-start.17 = (f32[96,1920]{1,0:T(8,128)S(1)}, f32[96,1920]{1,0:T(8,128)S(1)}, u32[]{:S(2)}, u32[]{:S(2)}) collective-permute-start(f32[96,1920]{1,0:T(8,128)S(1)} %bitcast_add_fusion.5), channel_id=1, source_target_pairs={{0,8},{2,10},{4,12},{6,14},{8,16},{10,18},{12,20},{14,22},{1,9},{3... | collective-permute-start | bytes 2211848 | tf_op jit(solution)/shard_map/ppermute | solution.py:511
  524.1 39.1 %collective-permute-start.25 = (f32[96,1536]{1,0:T(8,128)S(1)}, f32[96,1536]{1,0:T(8,128)S(1)}, u32[]{:S(2)}, u32[]{:S(2)}) collective-permute-start(f32[96,1536]{1,0:T(8,128)S(1)} %bitcast_add_fusion.15), channel_id=1, source_target_pairs={{0,8},{2,10},{4,12},{6,14},{8,16},{10,18},{12,20},{14,22},{1,9},{3... | collective-permute-start | bytes 1769480 | tf_op jit(solution)/shard_map/ppermute | solution.py:511
  534.9 34.3 %collective-permute-start.37 = (f32[96,1536]{1,0:T(8,128)S(1)}, f32[96,1536]{1,0:T(8,128)S(1)}, u32[]{:S(2)}, u32[]{:S(2)}) collective-permute-start(f32[96,1536]{1,0:T(8,128)S(1)} %get-tuple-element.344), channel_id=1, source_target_pairs={{16,8},{18,10},{20,12},{22,14},{24,16},{26,18},{28,20},{30,22},{17... | collective-permute-start | bytes 1769480 | tf_op jit(solution)/shard_map/ppermute | solution.py:514
  536.3 47.3 %collective-permute-start.35 = (f32[96,1536]{1,0:T(8,128)S(1)}, f32[96,1536]{1,0:T(8,128)S(1)}, u32[]{:S(2)}, u32[]{:S(2)}) collective-permute-start(f32[96,1536]{1,0:T(8,128)S(1)} %get-tuple-element.343), channel_id=1, source_target_pairs={{0,8},{2,10},{4,12},{6,14},{8,16},{10,18},{12,20},{14,22},{16,24},... | collective-permute-start | bytes 1769480 | tf_op jit(solution)/shard_map/ppermute | solution.py:511
  550.8 20.5 %collective-permute-start.20 = (f32[96,1920]{1,0:T(8,128)S(1)}, f32[96,1920]{1,0:T(8,128)S(1)}, u32[]{:S(2)}, u32[]{:S(2)}) collective-permute-start(f32[96,1920]{1,0:T(8,128)S(1)} %get-tuple-element.340), channel_id=1, source_target_pairs={{16,8},{18,10},{20,12},{22,14},{24,16},{26,18},{28,20},{30,22},{17... | collective-permute-start | bytes 2211848 | tf_op jit(solution)/shard_map/ppermute | solution.py:514
  563.4 18.2 %collective-permute-start.28 = (f32[96,1536]{1,0:T(8,128)S(1)}, f32[96,1536]{1,0:T(8,128)S(1)}, u32[]{:S(2)}, u32[]{:S(2)}) collective-permute-start(f32[96,1536]{1,0:T(8,128)S(1)} %get-tuple-element.348), channel_id=1, source_target_pairs={{16,8},{18,10},{20,12},{22,14},{24,16},{26,18},{28,20},{30,22},{17... | collective-permute-start | bytes 1769480 | tf_op jit(solution)/shard_map/ppermute | solution.py:514
  564.7 46.0 %collective-permute-start.26 = (f32[96,1536]{1,0:T(8,128)S(1)}, f32[96,1536]{1,0:T(8,128)S(1)}, u32[]{:S(2)}, u32[]{:S(2)}) collective-permute-start(f32[96,1536]{1,0:T(8,128)S(1)} %get-tuple-element.347), channel_id=1, source_target_pairs={{0,8},{2,10},{4,12},{6,14},{8,16},{10,18},{12,20},{14,22},{16,24},... | collective-permute-start | bytes 1769480 | tf_op jit(solution)/shard_map/ppermute | solution.py:511
  569.3 24.8 %collective-permute-start.38 = (f32[96,1536]{1,0:T(8,128)S(1)}, f32[96,1536]{1,0:T(8,128)S(1)}, u32[]{:S(2)}, u32[]{:S(2)}) collective-permute-start(f32[96,1536]{1,0:T(8,128)S(1)} %bitcast_add_fusion.9), channel_id=1, source_target_pairs={{8,0},{10,2},{12,4},{14,6},{16,8},{18,10},{20,12},{22,14},{24,16},... | collective-permute-start | bytes 1769480 | tf_op jit(solution)/shard_map/ppermute | solution.py:514
  571.3 29.1 %collective-permute-start.18 = (f32[96,1920]{1,0:T(8,128)S(1)}, f32[96,1920]{1,0:T(8,128)S(1)}, u32[]{:S(2)}, u32[]{:S(2)}) collective-permute-start(f32[96,1920]{1,0:T(8,128)S(1)} %get-tuple-element.339), channel_id=1, source_target_pairs={{0,8},{2,10},{4,12},{6,14},{8,16},{10,18},{12,20},{14,22},{16,24},... | collective-permute-start | bytes 2211848 | tf_op jit(solution)/shard_map/ppermute | solution.py:511
  581.5 28.4 %collective-permute-start.21 = (f32[96,1920]{1,0:T(8,128)S(1)}, f32[96,1920]{1,0:T(8,128)S(1)}, u32[]{:S(2)}, u32[]{:S(2)}) collective-permute-start(f32[96,1920]{1,0:T(8,128)S(1)} %bitcast_add_fusion.4), channel_id=1, source_target_pairs={{8,0},{10,2},{12,4},{14,6},{16,8},{18,10},{20,12},{22,14},{24,16},... | collective-permute-start | bytes 2211848 | tf_op jit(solution)/shard_map/ppermute | solution.py:514
  583.6 34.3 %collective-permute-start.29 = (f32[96,1536]{1,0:T(8,128)S(1)}, f32[96,1536]{1,0:T(8,128)S(1)}, u32[]{:S(2)}, u32[]{:S(2)}) collective-permute-start(f32[96,1536]{1,0:T(8,128)S(1)} %bitcast_add_fusion.14), channel_id=1, source_target_pairs={{8,0},{10,2},{12,4},{14,6},{16,8},{18,10},{20,12},{22,14},{24,16},... | collective-permute-start | bytes 1769480 | tf_op jit(solution)/shard_map/ppermute | solution.py:514
  610.1 10.2 %collective-permute-start.30 = (f32[48,256]{1,0:T(8,128)S(1)}, f32[48,256]{1,0:T(8,128)S(1)}, u32[]{:S(2)}, u32[]{:S(2)}) collective-permute-start(f32[48,256]{1,0:T(8,128)S(1)} %dynamic-slice_bitcast_fusion.13), channel_id=1, source_target_pairs={{0,1},{1,0},{2,3},{3,2},{4,5},{5,4},{6,7},{7,6},{8,9},{9,8},{10,11... | collective-permute-start | bytes 147464 | tf_op jit(solution)/shard_map/ppermute | solution.py:566
  (14 other events, 34.3 us)
